TPU v7x, 128 devices: a whole 4x4x4 slice. The times are simulated.
128 devices in a mesh: lon: 32 (over z, y_hi, x), lat: 2 (over core), dp: 2 (over y_lo).
Axes of the slice: x: 4, y: 4 (y_hi: 2, y_lo: 2; y = y_hi * 2 + y_lo), z: 4, core: 2. Of those that a mesh axis runs over, the one named last changes fastest.
Arguments:
- fields: bfloat16 [4, 3, 16, 640, 1024], P('dp', None, 'lat', 'lon'), may hold values from -6 to 6
- grad_y: bfloat16 [4, 3, 16, 640, 1024], P('dp', None, 'lat', 'lon'), may hold values from -6 to 6
- w_qkv: bfloat16 [1024, 3072], replicated
- w_out: bfloat16 [1024, 1024], replicated, may hold values from -0.1875 to 0.1875
- mask_ids: int32 [16, 640], replicated, may hold values from 0 to 2
Outputs:
- out_y: bfloat16 [4, 3, 16, 640, 1024], P('dp', None, 'lat', 'lon')
- grad_fields: bfloat16 [4, 3, 16, 640, 1024], P('dp', None, 'lat', 'lon')
- grad_w_qkv: float32 [1024, 3072], P('lon', ('lat', 'dp'))
- grad_w_out: float32 [1024, 1024], P('lon', ('lat', 'dp'))
All inputs are finite; a program needn't handle non-finite values.
Results may differ from a plain program's by a relative error of at most 0.033.
Values may be sent and summed in bfloat16 or wider, within the bound.
No kernel may reach another device: no remote copies, remote signals or barrier semaphores. Data moves between devices by JAX's collectives and lax.ppermute only.
A program may use at most 192 MiB of HBM per device.

v0:
```python
import functools

import jax
import jax.numpy as jnp
import numpy as np
from jax import lax
from jax.experimental import pallas as pl
from jax.experimental.pallas import tpu as pltpu
from jax.sharding import PartitionSpec as P

HEADS = 16
LEV = 3
WLAT = 4
WLON = 5
SLAT = 2
SLON = 2
ROWS = 8
COLS = 20
EPS = 1e-05

SIDE = 2 * WLON
GROUP = 128
HALF = 4 * GROUP
OWN = LEV * SIDE * ROWS
RIM = 128
COR = 16
BACK = 64
QUADS = 4
SCALE = 0.125
BF = jnp.bfloat16
F32 = jnp.float32
NT = (((1,), (1,)), ((), ()))

X, Y, Z = 4, 2, 4
UNIT = 32
LON, LAT = 0, 1


def params(mebibytes):
    return pltpu.CompilerParams(vmem_limit_bytes=mebibytes * 1024 * 1024)


def cost(micros):
    return pl.CostEstimate(flops=int(micros * 1.1e9), bytes_accessed=10**6, transcendentals=0)


SCALARS = pl.BlockSpec(memory_space=pltpu.SMEM)


def dot(a, b):
    return jnp.dot(a, b, preferred_element_type=F32)


def dot_nt(a, b):
    return lax.dot_general(a, b, NT, preferred_element_type=F32)


def place_of(lon):
    return lon % X, (lon // X) % Y, lon // (X * Y)


def relative(block, pos_ref):
    lon = pos_ref[LON]
    x, y, z = place_of(block)
    x0, y0, z0 = lax.rem(lon, X), lax.rem(lax.div(lon, X), Y), lax.div(lon, X * Y)
    dx, dy, dz = lax.rem(x - x0 + X, X), lax.rem(y - y0 + Y, Y), lax.rem(z - z0 + Z, Z)
    return (dx * Z + dz) * Y + dy


def token(level, r, c):
    return (level * WLAT + r) * SIDE + c


def every():
    for level in range(LEV):
        for c in range(SIDE):
            for i in range(ROWS):
                wr, r = divmod((i - SLAT) % ROWS, WLAT)
                yield level, c, i, wr, r


def one_hot(shape, places):
    out = np.zeros(shape, np.float32)
    for at in places:
        out[at] = 1.0
    return jnp.asarray(out.astype(jnp.bfloat16))


def pick_own():
    return one_hot(
        (2, GROUP, OWN),
        [
            (wr, token(level, r, c), (level * SIDE + c) * ROWS + i)
            for level, c, i, wr, r in every()
            if i >= SLAT
        ],
    )


def pick_rim(side):
    places = []
    for level, c, i, wr, r in every():
        if i < SLAT:
            column = SLON + side * SIDE + c
            if column < COLS:
                src = (level * COLS + column) * SLAT + i
            else:
                src = RIM + (level * SLON + column - COLS) * SLAT + i
            places.append((token(level, r, c), src))
    return one_hot((GROUP, RIM + COR), places)


def pick_out():
    return one_hot(
        (OWN, 2 * GROUP),
        [
            ((level * SIDE + c) * ROWS + i, wr * GROUP + token(level, r, c))
            for level, c, i, wr, r in every()
        ],
    )


def pick_back():
    return one_hot(
        (BACK, GROUP),
        [
            ((level * SIDE + c) * SLAT + i, token(level, r, c))
            for level, c, i, wr, r in every()
            if i < SLAT
        ],
    )


def pick_strip():
    rim = [
        ((level * COLS + column) * SLAT + i, (level * COLS + column) * ROWS + i)
        for level in range(LEV)
        for column in range(COLS)
        for i in range(SLAT)
    ]
    cor = [
        (RIM + (level * SLON + column) * SLAT + i, (level * COLS + column) * ROWS + i)
        for level in range(LEV)
        for column in range(SLON)
        for i in range(SLAT)
    ]
    return one_hot((RIM + COR, LEV * COLS * ROWS), rim + cor)


def pick_place(columns, start):
    return one_hot(
        (LEV, columns * ROWS, BACK),
        [
            (level, c * ROWS + i, (level * SIDE + start + c) * SLAT + i)
            for level in range(LEV)
            for c in range(columns)
            for i in range(SLAT)
        ],
    )


def strips_kernel(pick_ref, f_ref, g_ref, lon_ref, rim_ref, cor_ref):
    for arr, ref in enumerate((f_ref, g_ref)):
        block = ref[0]
        lon_ref[arr, 0] = block[:, : SLON * ROWS]
        strip = dot(pick_ref[...], block.reshape(-1, block.shape[-1])).astype(BF)
        rim_ref[arr, 0] = strip[:RIM]
        cor_ref[arr, 0] = strip[RIM:]


def strips(f, g):
    samples, levels, rows, width = f.shape
    pick = pick_strip()
    block = pl.BlockSpec((1, levels, rows, width), lambda b: (b, 0, 0, 0))
    shapes = [(levels, SLON * ROWS, width), (RIM, width), (COR, width)]
    return pl.pallas_call(
        strips_kernel,
        grid=(samples,),
        in_specs=[pl.BlockSpec(pick.shape, lambda b: (0, 0)), block, block],
        out_specs=[
            pl.BlockSpec((2, 1) + s, lambda b, n=len(s): (0, b) + (0,) * n) for s in shapes
        ],
        out_shape=[jax.ShapeDtypeStruct((2, samples) + s, BF) for s in shapes],
        compiler_params=params(56),
        cost_estimate=cost(3),
        name="strips",
    )(pick, f, g)


def project_kernel(
    side, pos_ref, own_ref, pick_ref, f_ref, g_ref, lon_ref, rim_ref, cor_ref, wq_ref, wk_ref, wv_ref, wo_ref,
    xw_ref, gw_ref, nt_ref, q_ref, k_ref, v_ref, da_ref, nw,
):
    samples, levels, _, width = f_ref.shape

    @pl.when(pl.program_id(0) == 0)
    def _():
        for b in range(samples):
            got = []
            for arr, ref in enumerate((f_ref, g_ref)):
                parts = []
                for level in range(levels):
                    if side == 0:
                        parts.append(ref[b, level, SLON * ROWS : (SLON + SIDE) * ROWS])
                    else:
                        parts.append(ref[b, level, (SLON + SIDE) * ROWS :])
                        parts.append(lon_ref[arr, b, level])
                own = jnp.concatenate(parts, axis=0)
                rim = jnp.concatenate([rim_ref[arr, b], cor_ref[arr, b]], axis=0)
                got.append((own, rim))
            for wr in range(2):
                at = slice((b * 2 + wr) * GROUP, (b * 2 + wr + 1) * GROUP)
                x, g = (dot(own_ref[wr], own) for own, _ in got)
                if wr == 1:
                    x, g = (a + dot(pick_ref[...], rim) for a, (_, rim) in zip((x, g), got))
                gw_ref[at, :] = g.astype(BF)
                xw_ref[at, :] = x.astype(BF)
                centred = x - jnp.mean(x, axis=-1, keepdims=True)
                inv = lax.rsqrt(jnp.mean(centred * centred, axis=-1, keepdims=True) + EPS)
                normed = (centred * inv).astype(BF)
                nw[at, :] = normed
                turned = normed.T
                for block in range(width // UNIT):
                    dst = pl.multiple_of(relative(block, pos_ref) * UNIT, UNIT)
                    nt_ref[pl.ds(dst, UNIT), at] = turned[block * UNIT : (block + 1) * UNIT]

    q_ref[...] = dot(nw[...], wq_ref[...]).astype(BF)
    k_ref[...] = dot(nw[...], wk_ref[...]).astype(BF)
    v_ref[...] = dot(nw[...], wv_ref[...]).astype(BF)
    da_ref[...] = dot_nt(gw_ref[...], wo_ref[...]).astype(BF)


def project(side, pos, f, g, lon_in, rim_in, cor_in, w_qkv, w_out):
    width = f.shape[-1]
    cols = width // QUADS
    whole = lambda n: (0, 0)
    full = lambda a: pl.BlockSpec(a.shape, lambda n: (0,) * a.ndim)
    own, pick = pick_own(), pick_rim(side)
    tall = jax.ShapeDtypeStruct((HALF, width), BF)
    return pl.pallas_call(
        functools.partial(project_kernel, side),
        grid=(QUADS,),
        in_specs=[
            pl.BlockSpec(memory_space=pltpu.SMEM),
            full(own),
            full(pick),
            full(f),
            full(g),
            full(lon_in),
            full(rim_in),
            full(cor_in),
            pl.BlockSpec((width, cols), lambda n: (0, n)),
            pl.BlockSpec((width, cols), lambda n: (0, QUADS + n)),
            pl.BlockSpec((width, cols), lambda n: (0, 2 * QUADS + n)),
            pl.BlockSpec((cols, width), lambda n: (n, 0)),
        ],
        out_specs=[
            pl.BlockSpec((HALF, width), whole),
            pl.BlockSpec((HALF, width), whole),
            pl.BlockSpec((width, HALF), whole),
        ]
        + [pl.BlockSpec((HALF, cols), lambda n: (0, n))] * 4,
        out_shape=[pltpu.HBM((HALF, width), BF), tall, jax.ShapeDtypeStruct((width, HALF), BF)] + [tall] * 4,
        scratch_shapes=[pltpu.VMEM((HALF, width), BF)],
        compiler_params=params(20),
        cost_estimate=cost(9),
        name="project",
    )(pos, own, pick, f, g, lon_in, rim_in, cor_in, w_qkv, w_qkv, w_qkv, w_out)


def attention_kernel(quads, pos_ref, bias_ref, *rest):
    sides, rest = (rest[:6], rest[6:12]), rest[12:]
    if quads == (3,):
        kin_ref, rest = rest[0], rest[1:]
    if quads == (1,):
        att_ref, dq_ref, dk_ref, dv_ref, keep_ref, send_ref, kout_ref, att_t = rest
    elif quads == (3,):
        att_ref, dq_ref, dk_ref, dv_ref, keep_ref, send_ref, att_t = rest
    else:
        att_ref, dq_ref, dk_ref, dv_ref, keep_ref, send_ref, gok_ref, gos_ref, att_t = rest
    width = sides[0][0].shape[0]
    cols = width // QUADS
    head = 64
    lat0 = pos_ref[LAT] == 0
    x0 = lax.rem(pos_ref[LON], X)
    first = lax.broadcasted_iota(jnp.int32, (GROUP, 2 * head), 1) < head
    upper = lax.broadcasted_iota(jnp.int32, (2 * head, GROUP), 0) < head
    zero = jnp.zeros((GROUP, 2 * head), BF)

    def split(pair):
        return jnp.concatenate([jnp.where(first, pair, zero), jnp.where(first, zero, pair)], axis=0)

    def beside(turned):
        return jnp.concatenate(
            [jnp.where(upper, turned, zero), jnp.where(upper, zero, turned)], axis=1
        )

    def stacked(both):
        return jnp.concatenate([both[:, :GROUP], both[:, GROUP:]], axis=0)

    def lanes(start, size):
        return pl.ds(start if isinstance(start, int) else pl.multiple_of(start, 128), size)

    def unit(refs, side, group, wr, pair, src, dst):
        _, _, q_ref, k_ref, v_ref, da_ref = refs
        at = (pl.ds(pl.multiple_of(group * GROUP, GROUP), GROUP), lanes(src + pair * 128, 128))
        here = pl.ds(pl.multiple_of(side * HALF + group * GROUP, GROUP), GROUP)
        both = lanes(dst + pair * 128, 128)
        bias = bias_ref[side * 2 + wr]
        q, k, v, da = q_ref[at], k_ref[at], v_ref[at], da_ref[at]
        q2, da2 = split(q * SCALE), split(da)
        scores = dot_nt(k, q2)
        d_prob = dot_nt(v, da2)
        yield
        scores = scores + jnp.concatenate([bias, bias], axis=1)
        top = jnp.max(scores, axis=0, keepdims=True)
        expd = jnp.exp(scores - top)
        prob = expd * (1.0 / jnp.sum(expd, axis=0, keepdims=True))
        prob16 = prob.astype(BF)
        part = prob * d_prob
        delta = jnp.sum(part, axis=0, keepdims=True)
        d_score = (part - prob * delta).astype(BF)
        yield
        out_t = dot(beside(v.T), stacked(prob16)).astype(BF)
        dq_t = dot(beside((k * SCALE).T), stacked(d_score)).astype(BF)
        dv_ref[here, both] = dot(prob16, da2).astype(BF)
        dk_ref[here, both] = dot(d_score, q2).astype(BF)
        yield
        att_ref[here, both] = out_t.T
        for block in range(128 // UNIT):
            row = lax.rem(block - x0 + X, X) * (2 * UNIT) + pair * UNIT
            att_t[pl.ds(pl.multiple_of(row, UNIT), UNIT), here] = out_t[
                block * UNIT : (block + 1) * UNIT
            ]
        dq_ref[here, both] = dq_t.T
        yield

    low, high = slice(0, HALF), slice(HALF, 2 * HALF)

    def units(src, dst):
        for side in range(2):

            def sample(b, carry):
                works = [
                    unit(sides[side], side, b * 2 + wr, wr, pair, src, dst)
                    for wr in range(2)
                    for pair in range(2)
                ]
                for _ in range(4):
                    for work in works:
                        next(work)
                return carry

            lax.fori_loop(0, HALF // (2 * GROUP), sample, 0)

    def out_sums():
        grad_out = dot(att_t[:, low], sides[0][1][...]) + dot(att_t[:, high], sides[1][1][...])
        left, right = grad_out[:, : width // 2], grad_out[:, width // 2 :]
        return jnp.where(lat0, left, right).astype(BF), jnp.where(lat0, right, left).astype(BF)

    def qkv_sums(store, dst):
        def piece(i, carry):
            at = pl.ds(pl.multiple_of(i * 256, 256), 256)
            left = (sides[0][0][at, :], sides[1][0][at, :])
            of_q, of_k, of_v = (
                dot(left[0], ref[low, lanes(dst, cols)]) + dot(left[1], ref[high, lanes(dst, cols)])
                for ref in (dq_ref, dk_ref, dv_ref)
            )
            mine = jnp.where(lat0, of_q, of_v).astype(BF)
            other = jnp.where(lat0, of_v, of_q).astype(BF)
            store(at, mine, other, of_k.astype(BF))
            return carry

        lax.fori_loop(0, width // 256, piece, 0)

    if quads == (0, 2):

        units(0, 0)
        gok_ref[...], gos_ref[...] = out_sums()
        n = pl.program_id(0)
        stays = jnp.logical_xor(lat0, n == 1)

        def store(at, mine, other, of_k):
            keep_ref[at, lanes(n * cols, cols)] = mine
            send_ref[at, lanes(n * cols, cols)] = other

            @pl.when(stays)
            def _():
                keep_ref[at, 2 * cols :] = of_k

            @pl.when(jnp.logical_not(stays))
            def _():
                send_ref[at, 2 * cols :] = of_k

        qkv_sums(store, 0)
        return

    units(0, 0)
    mine, other = out_sums()
    if quads == (1,):
        for half in range(2):
            below = slice(width + half * cols, width + (half + 1) * cols)
            keep_ref[below, :] = mine[:, half * cols : (half + 1) * cols]
            send_ref[below, :] = other[:, half * cols : (half + 1) * cols]
    else:
        keep_ref[width:, :] = mine
        send_ref[width:, :] = other

    def store(at, mine, other, of_k):
        keep_ref[at, :cols] = mine
        send_ref[at, :cols] = other
        if quads == (1,):
            kout_ref[at, :] = of_k
        else:
            before = kin_ref[at, :]
            keep_ref[at, cols:] = jnp.where(lat0, before, of_k)
            send_ref[at, cols:] = jnp.where(lat0, of_k, before)

    qkv_sums(store, 0)


def attention(quads, pos, bias, sides, before=None):
    width = sides[0][0].shape[1]
    cols = width // QUADS
    count = len(quads)
    rows = 2 * HALF

    def quad(n):
        return 2 * n if count == 2 else quads[0]

    whole = lambda n: (0, 0)
    in_specs = [SCALARS, pl.BlockSpec(bias.shape, lambda n: (0, 0, 0))]
    operands = [pos, bias]
    for _, gw, nt, q, k, v, da in sides:
        in_specs += [pl.BlockSpec((width, HALF), whole), pl.BlockSpec((HALF, width), whole)]
        in_specs += [pl.BlockSpec((HALF, cols), lambda n: (0, quad(n)))] * 4
        operands += [nt, gw, q, k, v, da]
    if before is not None:
        in_specs.append(pl.BlockSpec((width, cols), whole))
        operands.append(before)
    out_specs = [pl.BlockSpec((rows, cols), lambda n: (0, n))] * 4
    shapes = [(rows, count * cols)] * 4
    sums = {0: (width, 3 * cols), 1: (width + 2 * cols, cols), 3: (width + cols, 2 * cols)}[quads[0]]
    out_specs += [pl.BlockSpec(sums, whole)] * 2
    shapes += [sums] * 2
    if quads == (0, 2):
        out_specs += [pl.BlockSpec((cols, width // 2), lambda n: (n, 0))] * 2
        shapes += [(count * cols, width // 2)] * 2
    elif quads == (1,):
        out_specs += [pl.BlockSpec((width, cols), whole)]
        shapes += [(width, cols)]
    return pl.pallas_call(
        functools.partial(attention_kernel, quads),
        grid=(count,),
        in_specs=in_specs,
        out_specs=out_specs,
        out_shape=[pltpu.HBM(s, BF) if n < 4 and count == 2 else jax.ShapeDtypeStruct(s, BF) for n, s in enumerate(shapes)],
        scratch_shapes=[pltpu.VMEM((cols, 2 * HALF), BF)],
        compiler_params=params(20),
        cost_estimate=cost(11 * count),
        name="attention",
    )(*operands)


def output_kernel(side, out_ref, back_ref, x_ref, dy_ref, wqkv_ref, wo_ref, *rest):
    first, second, last = rest[:4], rest[4:8], rest[8:12]
    if side == 0:
        y_ref, gx_ref, rim_ref, branch_at, g_at = rest[12:]
    else:
        y_ref, gx_ref, rim_ref, lon_ref, branch_at, g_at = rest[12:]
    levels = y_ref.shape[1]
    cols = last[0].shape[1]
    step = pl.program_id(0)

    def by_quad(i):
        return [first[i][:, :cols], second[i][...], first[i][:, cols:], last[i][...]]

    branch_at[step] = dot(jnp.concatenate(by_quad(0), axis=1), wo_ref[...]).astype(BF)
    d_all = jnp.concatenate([a for i in (1, 2, 3) for a in by_quad(i)], axis=1)
    g_at[step] = dot_nt(d_all, wqkv_ref[...]).astype(BF)

    @pl.when(step == pl.num_programs(0) - 1)
    def _():
        def sample(b, carry):
            at = pl.ds(pl.multiple_of(b * 2 * GROUP, 2 * GROUP), 2 * GROUP)
            joined = lambda ref: jnp.concatenate([ref[n, at] for n in range(QUADS)], axis=1).astype(F32)
            x = x_ref[at, :].astype(F32)
            y = (x + joined(branch_at)).astype(BF)
            g = joined(g_at)
            centred = x - jnp.mean(x, axis=-1, keepdims=True)
            inv = lax.rsqrt(jnp.mean(centred * centred, axis=-1, keepdims=True) + EPS)
            normed = centred * inv
            gx = dy_ref[at, :].astype(F32) + inv * (
                g
                - jnp.mean(g, axis=-1, keepdims=True)
                - normed * jnp.mean(g * normed, axis=-1, keepdims=True)
            )
            for arr, (value, ref) in enumerate(((y, y_ref), (gx.astype(BF), gx_ref))):
                placed = dot(out_ref[...], value).astype(BF)
                back = dot(back_ref[...], value[GROUP:]).astype(BF)
                rim_ref[arr, b] = back
                kept = (SIDE if side == 0 else SIDE - SLON) * ROWS
                for level in range(levels):
                    start = level * SIDE * ROWS
                    ref[b, level] = placed[start : start + kept]
                    if side == 1:
                        lon_ref[arr, b, level] = placed[start + kept : start + SIDE * ROWS]
            return carry

        lax.fori_loop(0, HALF // (2 * GROUP), sample, 0)


def outputs(side, samples, xw, gw, w_qkv, w_out, first, second, last):
    width = w_out.shape[0]
    cols = width // QUADS
    out, back = pick_out(), pick_back()
    full = lambda shape: pl.BlockSpec(shape, lambda n: (0,) * len(shape))
    kept = (SIDE if side == 0 else SIDE - SLON) * ROWS
    shapes = [(samples, LEV, kept, width)] * 2 + [(2, samples, BACK, width)]
    if side == 1:
        shapes += [(2, samples, LEV, SLON * ROWS, width)]
    return pl.pallas_call(
        functools.partial(output_kernel, side),
        grid=(QUADS,),
        in_specs=[full(a.shape) for a in (out, back, xw, gw)]
        + [
            pl.BlockSpec((cols, 3 * width), lambda n: (n, 0)),
            pl.BlockSpec((width, cols), lambda n: (0, n)),
        ]
        + [pl.BlockSpec((HALF, 2 * cols), lambda n: (side, 0))] * 4
        + [pl.BlockSpec((HALF, cols), lambda n: (side, 0))] * 8,
        out_specs=[full(s) for s in shapes],
        out_shape=[jax.ShapeDtypeStruct(s, BF) for s in shapes],
        scratch_shapes=[pltpu.VMEM((QUADS, HALF, cols), BF)] * 2,
        compiler_params=params(14),
        cost_estimate=cost(8),
        name="outputs",
    )(out, back, xw, gw, w_qkv, w_out, *first[:4], *second[:4], *last[:4])


def replaced(mine, pick, rim):
    here = lax.broadcasted_iota(jnp.int32, mine.shape, 0) % ROWS < SLAT
    return jnp.where(here, dot(pick, rim).astype(BF), mine)


def patch_kernel(pick_ref, lon_ref, rim_ref, out_ref):
    for arr in range(2):
        for b in range(lon_ref.shape[1]):
            for level in range(lon_ref.shape[2]):
                out_ref[arr, b, level] = replaced(lon_ref[arr, b, level], pick_ref[level], rim_ref[arr, b])


def patch(lon, rim):
    return pl.pallas_call(
        patch_kernel,
        out_shape=jax.ShapeDtypeStruct(lon.shape, BF),
        compiler_params=params(12),
        cost_estimate=cost(1),
        name="patch",
    )(pick_place(SLON, SIDE - SLON), lon, rim)


def merge_kernel(place0_ref, place1_ref, y0, g0, y1, g1, rim0, rim1, lon, y_ref, gx_ref):
    levels = y_ref.shape[1]
    first, second = SLON * ROWS, (SLON + SIDE) * ROWS
    for arr, (low, high, out) in enumerate(((y0, y1, y_ref), (g0, g1, gx_ref))):
        for level in range(levels):
            out[0, level, :first] = lon[arr, 0, level]
            out[0, level, first:second] = replaced(low[0, level], place0_ref[level], rim0[arr, 0])
            out[0, level, second:] = replaced(high[0, level], place1_ref[level], rim1[arr, 0])


def merge(y0, g0, y1, g1, rim0, rim1, lon):
    samples, levels, _, width = y0.shape
    picks = [pick_place(SIDE, 0), pick_place(SIDE - SLON, 0)]
    full = lambda a: pl.BlockSpec(a.shape, lambda b: (0,) * a.ndim)
    own = lambda a: pl.BlockSpec((1,) + a.shape[1:], lambda b: (b,) + (0,) * (a.ndim - 1))
    strip = lambda a: pl.BlockSpec((2, 1) + a.shape[2:], lambda b: (0, b) + (0,) * (a.ndim - 2))
    shape = jax.ShapeDtypeStruct((samples, levels, COLS * ROWS, width), BF)
    return pl.pallas_call(
        merge_kernel,
        grid=(samples,),
        in_specs=[full(a) for a in picks]
        + [own(a) for a in (y0, g0, y1, g1)]
        + [strip(a) for a in (rim0, rim1, lon)],
        out_specs=[own(shape)] * 2,
        out_shape=[shape] * 2,
        compiler_params=params(12),
        cost_estimate=cost(4),
        name="merge",
    )(*picks, y0, g0, y1, g1, rim0, rim1, lon)


def shifted(value, axis, steps):
    count = lax.axis_size(axis)
    pairs = [(source, (source + steps) % count) for source in range(count)]
    return lax.ppermute(value, axis, pairs)


def shifted_both(value, steps):
    lon, lat = lax.axis_size("lon"), lax.axis_size("lat")
    pairs = [
        (i * lat + j, ((i + steps) % lon) * lat + (j + steps) % lat)
        for i in range(lon)
        for j in range(lat)
    ]
    return lax.ppermute(value, ("lon", "lat"), pairs)


def allowed_bias(mask_ids):
    lat_total = mask_ids.shape[0]
    start = lax.axis_index("lat") * ROWS + SLAT
    lat_global = (start + np.arange(ROWS, dtype=np.int32)) % lat_total
    wide = jnp.concatenate([mask_ids, mask_ids[:, :SLON]], axis=1)
    wide = jnp.concatenate([wide, wide[:SLAT]], axis=0)
    ids = lax.dynamic_slice(wide, (start, lax.axis_index("lon") * COLS + SLON), (ROWS, COLS))
    code = ids * 2 + (lat_global < SLAT).astype(jnp.int32)[:, None]
    code = code + 16 * (np.arange(COLS, dtype=np.int32) // WLON)[None, :]
    code = code.reshape(2, WLAT, 2, SIDE).transpose(2, 0, 1, 3).reshape(4, 1, WLAT * SIDE)
    code = jnp.broadcast_to(code, (4, LEV, WLAT * SIDE)).reshape(4, -1)
    code = jnp.pad(code, ((0, 0), (0, GROUP - code.shape[1])), constant_values=-1)
    same = code[:, :, None] == code[:, None, :]
    return jnp.where(same, 0.0, -jnp.inf).astype(F32)


def swapped(value, axis):
    return lax.ppermute(value, axis, [(0, 1), (1, 0)])


def to_distance(value, dx=0, dy=0, dz=0):
    pairs = []
    for lon in range(X * Y * Z):
        x, y, z = place_of(lon)
        pairs.append((lon, ((z + dz) % Z * Y + (y + dy) % Y) * X + (x + dx) % X))
    return lax.ppermute(value, "lon", pairs)


def added(*terms):
    total = terms[0].astype(F32)
    for term in terms[1:]:
        total = total + term.astype(F32)
    return total


def ring_sum(chunks, name):
    got = [to_distance(chunks[d], **{name: d}) for d in range(1, len(chunks))]
    return added(chunks[0], *got)


def relay(chunks, name):
    half = chunks[2].shape[0] // 2
    return [to_distance(chunks[2][:half], **{name: 1}), to_distance(chunks[2][half:], **{name: 3})]


def with_relayed(chunks, got):
    half = got[0].shape[0]
    up = jnp.concatenate([added(chunks[1][:half], got[0]).astype(BF), chunks[1][half:]], axis=0)
    down = jnp.concatenate([chunks[3][:half], added(chunks[3][half:], got[1]).astype(BF)], axis=0)
    return [up, down]


def both_ways(pair, name):
    return [to_distance(pair[0], **{name: 1}), to_distance(pair[1], **{name: 3})]


def swap_sum(keep, got):
    return added(keep, got).astype(BF)


def chunks_by_z(total):
    total = total.reshape(X, Z, Y * UNIT, -1)
    return [total[:, d].reshape(X * Y * UNIT, -1) for d in range(Z)]


def chunks_by_x(total):
    return jnp.split(total, X)


def chunks_with_out(qkv, outs):
    _, y0, z0 = place_of(lax.axis_index("lon"))
    outs = jnp.stack(outs).reshape(Z, X, Y, UNIT, -1)
    outs = jnp.where(y0 == 0, outs, outs[:, :, ::-1]).reshape(Z, X * Y * UNIT, -1)
    return [
        jnp.concatenate([chunk, lax.dynamic_index_in_dim(outs, (z0 + d) % Z, keepdims=False)], axis=1)
        for d, chunk in enumerate(chunks_by_z(qkv))
    ]


def final_sums(total):
    cols = total.shape[1] // 8
    piece = [total[:, i * cols : (i + 1) * cols] for i in range(8)]
    pick = lambda *which: jnp.concatenate([piece[i] for i in which], axis=1)
    lat0 = lax.axis_index("lat") == 0
    low = jnp.where(lat0, pick(0, 3, 1, 4), pick(2, 7, 0, 4))
    high = jnp.where(lat0, pick(6, 2, 7, 5), pick(3, 1, 6, 5))
    dp0 = lax.axis_index("dp") == 0
    got = swapped(jnp.where(dp0, high, low), "dp")
    total = added(jnp.where(dp0, low, high), got)
    return total[:, : 3 * cols], total[:, 3 * cols :]


def per_device(fields, grad_y, w_qkv, w_out, mask_ids):
    samples, levels, lat_rows, lon_cols, width = fields.shape
    flat = lambda a: a.transpose(0, 1, 3, 2, 4).reshape(samples, levels, lon_cols * lat_rows, width)
    f, g = flat(fields), flat(grad_y)
    pos = jnp.stack([lax.axis_index("lon"), lax.axis_index("lat")]).astype(jnp.int32)
    lon_out, rim_out, cor_out = strips(f, g)
    rim_in = shifted(rim_out, "lat", -1)
    cor_in = shifted_both(cor_out, -1)
    lon_in = shifted(lon_out, "lon", -1)
    bias = allowed_bias(mask_ids)
    side0 = project(0, pos, f, g, lon_out, rim_in, cor_out, w_qkv, w_out)
    side1 = project(1, pos, f, g, lon_in, rim_in, cor_in, w_qkv, w_out)
    sides = (side0, side1)
    barrier = lax.optimization_barrier
    first = attention((0, 2), pos, bias, sides)
    by_z = chunks_by_z(swap_sum(first[4], swapped(first[5], "lat")))
    outs = swap_sum(first[6], swapped(first[7], "lat"))
    by_z, pos1 = barrier((by_z, pos))
    got_z = relay(by_z, "dz")
    second = attention((1,), pos1, bias, sides)
    got_z, before, send = barrier((got_z, second[6], second[5]))
    ways, before = barrier((with_relayed(by_z, got_z), before))
    got_z = both_ways(ways, "dz")
    last = attention((3,), pos, bias, sides, before=before)
    got_z, send, send_last = barrier((got_z, send, last[5]))
    first_total = added(by_z[0], *got_z).astype(BF).reshape(X, Y * UNIT, -1)
    got, got_last = swapped(send, "lat"), swapped(send_last, "lat")
    total = swap_sum(second[4], got)
    cols = total.shape[1]
    out = jnp.concatenate([total[-2 * cols : -cols], total[-cols:]], axis=1)
    total_last = swap_sum(last[4], got_last)
    outs = [outs[:cols], out, outs[cols:], total_last[-cols:]]
    by_x = chunks_by_x(total_last[:-cols])
    by_z = chunks_with_out(total[: -2 * cols], outs)
    by_x, by_z, att = barrier((by_x, by_z, last[0]))
    got_x, got_z = relay(by_x, "dx"), relay(by_z, "dz")
    last = (att, *last[1:])
    y1, g1, rim1, lon = outputs(1, samples, *side1[:2], w_qkv, w_out, first, second, last)
    rim1 = shifted(rim1, "lat", 1)
    got_x, got_z, lon = barrier((got_x, got_z, lon))
    ways_x, ways_z = with_relayed(by_x, got_x), with_relayed(by_z, got_z)
    lon = patch(lon, rim1)
    ways_x, ways_z, lon, xw0 = barrier((ways_x, ways_z, lon, side0[0]))
    got_x, got_z = both_ways(ways_x, "dx"), both_ways(ways_z, "dz")
    lon = shifted(lon, "lon", 1)
    y0, g0, rim0 = outputs(0, samples, xw0, side0[1], w_qkv, w_out, first, second, last)
    got_x, got_z, rim0 = barrier((got_x, got_z, rim0))
    rim0 = shifted(rim0, "lat", 1)
    by_z_own = by_z[0]
    by_z = added(by_x[0], *got_x).astype(BF).reshape(Z, Y * UNIT, -1)
    total_z = added(by_z_own, *got_z).astype(BF).reshape(X, Y * UNIT, -1)
    by_x = [jnp.concatenate([first_total[d], total_z[d]], axis=1) for d in range(X)]
    total_z = ring_sum(list(by_z), "dz")
    total = jnp.concatenate([ring_sum(by_x, "dx").astype(BF), total_z.astype(BF)], axis=1)
    total = total.reshape(Y, UNIT, -1)
    got_y = to_distance(total[1], dy=1)
    y, gx = merge(y0, g0, y1, g1, rim0, rim1, lon)
    got_y, y, gx = barrier((got_y, y, gx))
    sums = final_sums(added(total[0], got_y).astype(BF))
    unflat = lambda a: a.reshape(samples, levels, lon_cols, lat_rows, width).transpose(0, 1, 3, 2, 4)
    return (unflat(y), unflat(gx), *sums)


def solution(mesh):
    grid = P("dp", None, "lat", "lon", None)
    return jax.shard_map(
        per_device,
        mesh=mesh,
        in_specs=(grid, grid, P(), P(), P()),
        out_specs=(grid, grid, P("lon", ("lat", "dp")), P("lon", ("lat", "dp"))),
        check_vma=False,
    )
```

profile of v0, /device:TPU:64, one launch (start us, length us, event | category | flops | bytes accessed | tf_op | source)
XLA Modules:
  0.0 159.3 jit_solution(10324134720831313022)
XLA Ops:
  0.7 3.6 %strips.1 = (bf16[2,2,3,16,1024]{4,3,2,1,0:T(8,128)(2,1)}, bf16[2,2,128,1024]{3,2,1,0:T(8,128)(2,1)}, bf16[2,2,16,1024]{3,2,1,0:T(8,128)(2,1)}) custom-call(bf16[144,480]{1,0:T(8,128)(2,1)} %constant.132.clone.pick_ref, bf16[2,3,160,1024]{3,2,1,0:T(8,128)(2,1)} %bitcast.42, bf16[2,3,160,1024]{3,2,1,0:T(8,128)(2,1)} %bitcast.45), custom_call_target="tpu_custom_call" | custom-call | flops 3300000000 | bytes 1000000 | tf_op jit(solution)/shard_map/strips/pallas_call | solution.py:176
  4.3 5.1 %collective-permute-start.2 = (bf16[2,2,16,1024]{3,2,1,0:T(8,128)(2,1)}, bf16[2,2,16,1024]{3,2,1,0:T(8,128)(2,1)S(1)}, u32[]{:S(2)}, u32[]{:S(2)}) collective-permute-start(bf16[2,2,16,1024]{3,2,1,0:T(8,128)(2,1)} %get-tuple-element.97.cor_ref), channel_id=1, source_target_pairs={{0,126},{2,124},{4,2},{6,0},{8,6},{10,4},{12,10},{14,8},{16,14},{1... | collective-permute-start | bytes 393224 | tf_op jit(solution)/shard_map/ppermute | solution.py:607
  10.8 2.8 %copy-done = bf16[1024,3072]{1,0:T(8,128)(2,1)S(1)} copy-done((bf16[1024,3072]{1,0:T(8,128)(2,1)S(1)}, bf16[1024,3072]{1,0:T(8,128)(2,1)}, u32[]{:S(2)}) %copy-start) | copy-done | bytes 6291480
  20.4 8.6 %project.2 = (bf16[512,1024]{1,0:T(8,128)(2,1)}, bf16[512,1024]{1,0:T(8,128)(2,1)S(1)}, bf16[1024,512]{1,0:T(8,128)(2,1)S(1)}, bf16[512,1024]{1,0:T(8,128)(2,1)S...) custom-call(s32[2]{0:T(128)S(1)} %pad_add_fusion.1.pos_ref, ...), custom_call_target="tpu_custom_call" | custom-call | flops 9900000256 | bytes 1000000 | tf_op jit(solution)/shard_map/project/pallas_call | solution.py:240
  29.1 9.4 %project.3 = (bf16[512,1024]{1,0:T(8,128)(2,1)}, bf16[512,1024]{1,0:T(8,128)(2,1)S(1)}, bf16[1024,512]{1,0:T(8,128)(2,1)S(1)}, bf16[512,1024]{1,0:T(8,128)(2,1)S...) custom-call(s32[2]{0:T(128)S(1)} %pad_add_fusion.1.pos_ref, ...), custom_call_target="tpu_custom_call" | custom-call | flops 9900000256 | bytes 1000000 | tf_op jit(solution)/shard_map/project/pallas_call | solution.py:240
  38.6 15.9 %attention.3 = (bf16[1024,512]{1,0:T(8,128)(2,1)}, bf16[1024,512]{1,0:T(8,128)(2,1)}, bf16[1024,512]{1,0:T(8,128)(2,1)}, bf16[1024,512]{1,0:T(8,128)(2,1)}, bf16...) custom-call(s32[2]{0:T(128)S(1)} %pad_add_fusion.1.pos_ref, ...), custom_call_target="tpu_custom_call" | custom-call | flops 24199999488 | bytes 1000000 | tf_op jit(solution)/shard_map/attention/pallas_call | solution.py:452
  55.1 3.2 %collective-permute-done.3 = bf16[1024,768]{1,0:T(8,128)(2,1)} collective-permute-done((bf16[1024,768]{1,0:T(8,128)(2,1)}, bf16[1024,768]{1,0:T(8,128)(2,1)}, u32[]{:S(2)}, u32[]{:S(2)}) %collective-permute-start.3) | collective-permute-done | bytes 1572896 | tf_op jit(solution)/shard_map/ppermute | solution.py:627
  58.4 1.9 %add_convert_fusion = bf16[1024,768]{1,0:T(8,128)(2,1)S(1)} fusion(bf16[1024,768]{1,0:T(8,128)(2,1)} %collective-permute-done.3, bf16[1024,768]{1,0:T(8,128)(2,1)S(1)} %get-tuple-element.110), kind=kLoop, calls=%fused_computation | loop fusion | flops 3145728 | bytes 4718592 | tf_op jit(solution)/shard_map/convert_element_type | solution.py:667
  67.8 7.0 %attention.4 = (bf16[1024,256]{1,0:T(8,128)(2,1)S(1)}, bf16[1024,256]{1,0:T(8,128)(2,1)S(1)}, bf16[1024,256]{1,0:T(8,128)(2,1)S(1)}, bf16[1024,256]{1,0:T(8,128)...) custom-call(s32[2]{0:T(128)S(1)} %pad_add_fusion.1.pos_ref, ...), custom_call_target="tpu_custom_call" | custom-call | flops 12099999744 | bytes 1000000 | tf_op jit(solution)/shard_map/attention/pallas_call | solution.py:452
  75.0 3.2 %collective-permute-start.6 = (bf16[256,768]{1,0:T(8,128)(2,1)S(1)}, bf16[256,768]{1,0:T(8,128)(2,1)S(1)}, u32[]{:S(2)}, u32[]{:S(2)}) collective-permute-start(bf16[256,768]{1,0:T(8,128)(2,1)S(1)} %pad_maximum_fusion.1), channel_id=1, source_target_pairs={{0,32},{4,36},{8,40},{12,44},{16,48},{20,52},{24,56},{28,60},{32,6... | collective-permute-start | bytes 1179656 | tf_op jit(solution)/shard_map/ppermute | solution.py:635
  78.3 7.0 %attention.5 = (bf16[1024,256]{1,0:T(8,128)(2,1)S(1)}, bf16[1024,256]{1,0:T(8,128)(2,1)S(1)}, bf16[1024,256]{1,0:T(8,128)(2,1)S(1)}, bf16[1024,256]{1,0:T(8,128)...) custom-call(s32[2]{0:T(128)S(1)} %pad_add_fusion.1.pos_ref, ...), custom_call_target="tpu_custom_call" | custom-call | flops 12099999744 | bytes 1000000 | tf_op jit(solution)/shard_map/attention/pallas_call | solution.py:452
  86.4 2.2 %collective-permute-done.7 = bf16[256,768]{1,0:T(8,128)(2,1)S(1)} collective-permute-done((bf16[256,768]{1,0:T(8,128)(2,1)S(1)}, bf16[256,768]{1,0:T(8,128)(2,1)S(1)}, u32[]{:S(2)}, u32[]{:S(2)}) %collective-permute-start.7) | collective-permute-done | bytes 393248 | tf_op jit(solution)/shard_map/ppermute | solution.py:635
  94.2 2.0 %collective-permute-start.11 = (bf16[128,512]{1,0:T(8,128)(2,1)S(1)}, bf16[128,512]{1,0:T(8,128)(2,1)S(1)}, u32[]{:S(2)}, u32[]{:S(2)}) collective-permute-start(bf16[128,512]{1,0:T(8,128)(2,1)S(1)} %get-tuple-element.223), channel_id=1, source_target_pairs={{0,4},{4,8},{8,12},{12,0},{16,20},{20,24},{24,28},{28,16},{32,36},... | collective-permute-start | bytes 393224 | tf_op jit(solution)/shard_map/ppermute | solution.py:635
  96.5 3.0 %collective-permute-start.13 = (bf16[128,768]{1,0:T(8,128)(2,1)S(1)}, bf16[128,768]{1,0:T(8,128)(2,1)S(1)}, u32[]{:S(2)}, u32[]{:S(2)}) collective-permute-start(bf16[128,768]{1,0:T(8,128)(2,1)S(1)} %get-tuple-element.216), channel_id=1, source_target_pairs={{0,32},{4,36},{8,40},{12,44},{16,48},{20,52},{24,56},{28,60},{32,6... | collective-permute-start | bytes 589832 | tf_op jit(solution)/shard_map/ppermute | solution.py:635
  99.6 7.7 %outputs.2 = (bf16[2,3,64,1024]{3,2,1,0:T(8,128)(2,1)S(1)}, bf16[2,3,64,1024]{3,2,1,0:T(8,128)(2,1)S(1)}, bf16[2,2,64,1024]{3,2,1,0:T(8,128)(2,1)S(1)}, bf16[2,2,3,16,1024]{4,3,2,1,0:T(8,128)(2,1)S(1)}) custom-call(bf16[240,256]{1,0:T(8,128)(2,1)S(1)} %copy-done.9, bf16[64,128]{1,0:T(8,128)(2,1)S(1)} %copy-done.14, bf16[512,1024]{1,0:T(8,128)(2,1)S(1)} %copy-done.19, ...), custom_call_target="tpu_custom_call" | custom-call | flops 8800000000 | bytes 1000000 | tf_op jit(solution)/shard_map/outputs/pallas_call | solution.py:522
  111.0 2.0 %collective-permute-start.17 = (bf16[256,512]{1,0:T(8,128)(2,1)S(1)}, bf16[256,512]{1,0:T(8,128)(2,1)S(1)}, u32[]{:S(2)}, u32[]{:S(2)}) collective-permute-start(bf16[256,512]{1,0:T(8,128)(2,1)S(1)} %pad_maximum_fusion.11), channel_id=1, source_target_pairs={{0,12},{4,0},{8,4},{12,8},{16,28},{20,16},{24,20},{28,24},{32,44},... | collective-permute-start | bytes 786440 | tf_op jit(solution)/shard_map/ppermute | solution.py:635
  113.0 2.9 %collective-permute-start.18 = (bf16[256,768]{1,0:T(8,128)(2,1)S(1)}, bf16[256,768]{1,0:T(8,128)(2,1)S(1)}, u32[]{:S(2)}, u32[]{:S(2)}) collective-permute-start(bf16[256,768]{1,0:T(8,128)(2,1)S(1)} %pad_maximum_fusion.7), channel_id=1, source_target_pairs={{0,32},{4,36},{8,40},{12,44},{16,48},{20,52},{24,56},{28,60},{32,6... | collective-permute-start | bytes 1179656 | tf_op jit(solution)/shard_map/ppermute | solution.py:635
  115.9 7.7 %outputs.3 = (bf16[2,3,80,1024]{3,2,1,0:T(8,128)(2,1)S(1)}, bf16[2,3,80,1024]{3,2,1,0:T(8,128)(2,1)S(1)}, bf16[2,2,64,1024]{3,2,1,0:T(8,128)(2,1)S(1)}) custom-call(bf16[240,256]{1,0:T(8,128)(2,1)S(1)} %copy-done.9, bf16[64,128]{1,0:T(8,128)(2,1)S(1)} %copy-done.14, bf16[512,1024]{1,0:T(8,128)(2,1)S(1)} %copy-done.16, bf16[512,1024]{1,0:T(8,128)(2,1)S(1)} %copy-done.18, ...), custom_call_target="tpu_custom_call" | custom-call | flops 8800000000 | bytes 1000000 | tf_op jit(solution)/shard_map/outputs/pallas_call | solution.py:522
  124.1 2.2 %collective-permute-done.19 = bf16[256,768]{1,0:T(8,128)(2,1)S(1)} collective-permute-done((bf16[256,768]{1,0:T(8,128)(2,1)S(1)}, bf16[256,768]{1,0:T(8,128)(2,1)S(1)}, u32[]{:S(2)}, u32[]{:S(2)}) %collective-permute-start.19) | collective-permute-done | bytes 393248 | tf_op jit(solution)/shard_map/ppermute | solution.py:635
  130.7 9.0 %collective-permute-done.23 = bf16[64,512]{1,0:T(8,128)(2,1)S(1)} collective-permute-done((bf16[64,512]{1,0:T(8,128)(2,1)S(1)}, bf16[64,512]{1,0:T(8,128)(2,1)S(1)}, u32[]{:S(2)}, u32[]{:S(2)}) %collective-permute-start.23) | collective-permute-done | bytes 65568 | tf_op jit(solution)/shard_map/ppermute | solution.py:635
  139.9 7.0 %collective-permute-done.21 = bf16[64,1536]{1,0:T(8,128)(2,1)S(1)} collective-permute-done((bf16[64,1536]{1,0:T(8,128)(2,1)S(1)}, bf16[64,1536]{1,0:T(8,128)(2,1)S(1)}, u32[]{:S(2)}, u32[]{:S(2)}) %collective-permute-start.21) | collective-permute-done | bytes 196640 | tf_op jit(solution)/shard_map/ppermute | solution.py:635
  148.0 2.6 %merge.1 = (bf16[2,3,160,1024]{3,2,1,0:T(8,128)(2,1)}, bf16[2,3,160,1024]{3,2,1,0:T(8,128)(2,1)}) custom-call(bf16[3,80,64]{2,1,0:T(8,128)(2,1)S(1)} %copy-done.12, bf16[3,64,64]{2,1,0:T(8,128)(2,1)S(1)} %copy-done.13, bf16[2,3,80,1024]{3,2,1,0:T(8,128)(2,1)S(1)} %get-tuple-element.175.y0, bf16[2,3,80,1024]{3,2,1,0:T(8,128)(2,1)S(1)} %get-tuple-element.176.g0, ...), custom_call_target="tpu_custom_call" | custom-call | flops 4400000000 | bytes 1000000 | tf_op jit(solution)/shard_map/merge/pallas_call | solution.py:580
  150.7 2.9 %collective-permute-done.26 = bf16[32,2048]{1,0:T(8,128)(2,1)S(1)} collective-permute-done((bf16[32,2048]{1,0:T(8,128)(2,1)S(1)}, bf16[32,2048]{1,0:T(8,128)(2,1)S(1)}, u32[]{:S(2)}, u32[]{:S(2)}) %collective-permute-start.26) | collective-permute-done | bytes 131104 | tf_op jit(solution)/shard_map/ppermute | solution.py:635
  155.0 3.0 %collective-permute-done.29 = bf16[32,1024]{1,0:T(8,128)(2,1)S(1)} collective-permute-done((bf16[32,1024]{1,0:T(8,128)(2,1)S(1)}, bf16[32,1024]{1,0:T(8,128)(2,1)S(1)}, u32[]{:S(2)}, u32[]{:S(2)}) %collective-permute-start.29) | collective-permute-done | bytes 65568 | tf_op jit(solution)/shard_map/ppermute | solution.py:627
  (226 shorter events, 35.3 us)
Async XLA Ops:
  4.3 24.7 %collective-permute-start.2 = (bf16[2,2,16,1024]{3,2,1,0:T(8,128)(2,1)}, bf16[2,2,16,1024]{3,2,1,0:T(8,128)(2,1)S(1)}, u32[]{:S(2)}, u32[]{:S(2)}) collective-permute-start(bf16[2,2,16,1024]{3,2,1,0:T(8,128)(2,1)} %get-tuple-element.97.cor_ref), channel_id=1, source_target_pairs={{0,126},{2,124},{4,2},{6,0},{8,6},{10,4},{12,10},{14,8},{16,14},{1... | collective-permute-start | bytes 393224 | tf_op jit(solution)/shard_map/ppermute | solution.py:607
  9.4 19.7 %collective-permute-start.1 = (bf16[2,2,3,16,1024]{4,3,2,1,0:T(8,128)(2,1)}, bf16[2,2,3,16,1024]{4,3,2,1,0:T(8,128)(2,1)}, u32[]{:S(2)}, u32[]{:S(2)}) collective-permute-start(bf16[2,2,3,16,1024]{4,3,2,1,0:T(8,128)(2,1)} %get-tuple-element.95.lon_ref), channel_id=1, source_target_pairs={{0,124},{4,0},{8,4},{12,8},{16,12},{20,16},{24,20},{28,24},{32,28}... | collective-permute-start | bytes 1179656 | tf_op jit(solution)/shard_map/ppermute | solution.py:597
  54.8 33.9 %collective-permute-start.10 = (bf16[512,512]{1,0:T(8,128)(2,1)S(1)}, bf16[512,512]{1,0:T(8,128)(2,1)S(1)}, u32[]{:S(2)}, u32[]{:S(2)}) collective-permute-start(bf16[512,512]{1,0:T(8,128)(2,1)S(1)} %get-tuple-element.134), channel_id=1, source_target_pairs={{0,2},{2,0},{1,3},{3,1},{4,6},{6,4},{5,7},{7,5},{8,10},{10,8},{9,1... | collective-permute-start | bytes 1572872 | tf_op jit(solution)/shard_map/ppermute | solution.py:627
  60.5 14.3 %collective-permute-start.5 = (bf16[128,768]{1,0:T(8,128)(2,1)S(1)}, bf16[128,768]{1,0:T(8,128)(2,1)S(1)}, u32[]{:S(2)}, u32[]{:S(2)}) collective-permute-start(bf16[128,768]{1,0:T(8,128)(2,1)S(1)} %get-tuple-element.217), channel_id=1, source_target_pairs={{0,96},{4,100},{8,104},{12,108},{16,112},{20,116},{24,120},{28,124... | collective-permute-start | bytes 589832 | tf_op jit(solution)/shard_map/ppermute | solution.py:635
  60.9 14.0 %collective-permute-start.4 = (bf16[128,768]{1,0:T(8,128)(2,1)S(1)}, bf16[128,768]{1,0:T(8,128)(2,1)S(1)}, u32[]{:S(2)}, u32[]{:S(2)}) collective-permute-start(bf16[128,768]{1,0:T(8,128)(2,1)S(1)} %get-tuple-element.218), channel_id=1, source_target_pairs={{0,32},{4,36},{8,40},{12,44},{16,48},{20,52},{24,56},{28,60},{32,6... | collective-permute-start | bytes 589832 | tf_op jit(solution)/shard_map/ppermute | solution.py:635
  75.0 11.3 %collective-permute-start.6 = (bf16[256,768]{1,0:T(8,128)(2,1)S(1)}, bf16[256,768]{1,0:T(8,128)(2,1)S(1)}, u32[]{:S(2)}, u32[]{:S(2)}) collective-permute-start(bf16[256,768]{1,0:T(8,128)(2,1)S(1)} %pad_maximum_fusion.1), channel_id=1, source_target_pairs={{0,32},{4,36},{8,40},{12,44},{16,48},{20,52},{24,56},{28,60},{32,6... | collective-permute-start | bytes 1179656 | tf_op jit(solution)/shard_map/ppermute | solution.py:635
  78.3 10.4 %collective-permute-start.7 = (bf16[256,768]{1,0:T(8,128)(2,1)S(1)}, bf16[256,768]{1,0:T(8,128)(2,1)S(1)}, u32[]{:S(2)}, u32[]{:S(2)}) collective-permute-start(bf16[256,768]{1,0:T(8,128)(2,1)S(1)} %pad_maximum_fusion.2), channel_id=1, source_target_pairs={{0,96},{4,100},{8,104},{12,108},{16,112},{20,116},{24,120},{28,124... | collective-permute-start | bytes 1179656 | tf_op jit(solution)/shard_map/ppermute | solution.py:635
  94.1 13.4 %collective-permute-start.12 = (bf16[128,512]{1,0:T(8,128)(2,1)S(1)}, bf16[128,512]{1,0:T(8,128)(2,1)S(1)}, u32[]{:S(2)}, u32[]{:S(2)}) collective-permute-start(bf16[128,512]{1,0:T(8,128)(2,1)S(1)} %get-tuple-element.222), channel_id=1, source_target_pairs={{0,12},{4,0},{8,4},{12,8},{16,28},{20,16},{24,20},{28,24},{32,44},... | collective-permute-start | bytes 393224 | tf_op jit(solution)/shard_map/ppermute | solution.py:635
  94.2 13.3 %collective-permute-start.11 = (bf16[128,512]{1,0:T(8,128)(2,1)S(1)}, bf16[128,512]{1,0:T(8,128)(2,1)S(1)}, u32[]{:S(2)}, u32[]{:S(2)}) collective-permute-start(bf16[128,512]{1,0:T(8,128)(2,1)S(1)} %get-tuple-element.223), channel_id=1, source_target_pairs={{0,4},{4,8},{8,12},{12,0},{16,20},{20,24},{24,28},{28,16},{32,36},... | collective-permute-start | bytes 393224 | tf_op jit(solution)/shard_map/ppermute | solution.py:635
  96.2 11.3 %collective-permute-start.14 = (bf16[128,768]{1,0:T(8,128)(2,1)S(1)}, bf16[128,768]{1,0:T(8,128)(2,1)S(1)}, u32[]{:S(2)}, u32[]{:S(2)}) collective-permute-start(bf16[128,768]{1,0:T(8,128)(2,1)S(1)} %get-tuple-element.215), channel_id=1, source_target_pairs={{0,96},{4,100},{8,104},{12,108},{16,112},{20,116},{24,120},{28,124... | collective-permute-start | bytes 589832 | tf_op jit(solution)/shard_map/ppermute | solution.py:635
  96.5 11.0 %collective-permute-start.13 = (bf16[128,768]{1,0:T(8,128)(2,1)S(1)}, bf16[128,768]{1,0:T(8,128)(2,1)S(1)}, u32[]{:S(2)}, u32[]{:S(2)}) collective-permute-start(bf16[128,768]{1,0:T(8,128)(2,1)S(1)} %get-tuple-element.216), channel_id=1, source_target_pairs={{0,32},{4,36},{8,40},{12,44},{16,48},{20,52},{24,56},{28,60},{32,6... | collective-permute-start | bytes 589832 | tf_op jit(solution)/shard_map/ppermute | solution.py:635
  109.7 14.0 %collective-permute-start.16 = (bf16[256,512]{1,0:T(8,128)(2,1)S(1)}, bf16[256,512]{1,0:T(8,128)(2,1)S(1)}, u32[]{:S(2)}, u32[]{:S(2)}) collective-permute-start(bf16[256,512]{1,0:T(8,128)(2,1)S(1)} %pad_maximum_fusion.10), channel_id=1, source_target_pairs={{0,4},{4,8},{8,12},{12,0},{16,20},{20,24},{24,28},{28,16},{32,36},... | collective-permute-start | bytes 786440 | tf_op jit(solution)/shard_map/ppermute | solution.py:635
  111.0 12.8 %collective-permute-start.17 = (bf16[256,512]{1,0:T(8,128)(2,1)S(1)}, bf16[256,512]{1,0:T(8,128)(2,1)S(1)}, u32[]{:S(2)}, u32[]{:S(2)}) collective-permute-start(bf16[256,512]{1,0:T(8,128)(2,1)S(1)} %pad_maximum_fusion.11), channel_id=1, source_target_pairs={{0,12},{4,0},{8,4},{12,8},{16,28},{20,16},{24,20},{28,24},{32,44},... | collective-permute-start | bytes 786440 | tf_op jit(solution)/shard_map/ppermute | solution.py:635
  113.0 11.0 %collective-permute-start.18 = (bf16[256,768]{1,0:T(8,128)(2,1)S(1)}, bf16[256,768]{1,0:T(8,128)(2,1)S(1)}, u32[]{:S(2)}, u32[]{:S(2)}) collective-permute-start(bf16[256,768]{1,0:T(8,128)(2,1)S(1)} %pad_maximum_fusion.7), channel_id=1, source_target_pairs={{0,32},{4,36},{8,40},{12,44},{16,48},{20,52},{24,56},{28,60},{32,6... | collective-permute-start | bytes 1179656 | tf_op jit(solution)/shard_map/ppermute | solution.py:635
  115.9 10.3 %collective-permute-start.19 = (bf16[256,768]{1,0:T(8,128)(2,1)S(1)}, bf16[256,768]{1,0:T(8,128)(2,1)S(1)}, u32[]{:S(2)}, u32[]{:S(2)}) collective-permute-start(bf16[256,768]{1,0:T(8,128)(2,1)S(1)} %pad_maximum_fusion.8), channel_id=1, source_target_pairs={{0,96},{4,100},{8,104},{12,108},{16,112},{20,116},{24,120},{28,124... | collective-permute-start | bytes 1179656 | tf_op jit(solution)/shard_map/ppermute | solution.py:635
  123.6 24.4 %collective-permute-start.28 = (bf16[2,2,3,16,1024]{4,3,2,1,0:T(8,128)(2,1)S(1)}, bf16[2,2,3,16,1024]{4,3,2,1,0:T(8,128)(2,1)S(1)}, u32[]{:S(2)}, u32[]{:S(2)}) collective-permute-start(bf16[2,2,3,16,1024]{4,3,2,1,0:T(8,128)(2,1)S(1)} %patch.1), channel_id=1, source_target_pairs={{0,4},{4,8},{8,12},{12,16},{16,20},{20,24},{24,28},{28,32},{32,36}... | collective-permute-start | bytes 1179656 | tf_op jit(solution)/shard_map/ppermute | solution.py:597
  126.6 13.1 %collective-permute-start.23 = (bf16[64,512]{1,0:T(8,128)(2,1)S(1)}, bf16[64,512]{1,0:T(8,128)(2,1)S(1)}, u32[]{:S(2)}, u32[]{:S(2)}) collective-permute-start(bf16[64,512]{1,0:T(8,128)(2,1)S(1)} %get-tuple-element.219), channel_id=1, source_target_pairs={{0,32},{4,36},{8,40},{12,44},{16,48},{20,52},{24,56},{28,60},{32,6... | collective-permute-start | bytes 196616 | tf_op jit(solution)/shard_map/ppermute | solution.py:635
  128.2 11.5 %collective-permute-start.25 = (bf16[64,512]{1,0:T(8,128)(2,1)S(1)}, bf16[64,512]{1,0:T(8,128)(2,1)S(1)}, u32[]{:S(2)}, u32[]{:S(2)}) collective-permute-start(bf16[64,512]{1,0:T(8,128)(2,1)S(1)} %get-tuple-element.220), channel_id=1, source_target_pairs={{0,96},{4,100},{8,104},{12,108},{16,112},{20,116},{24,120},{28,124... | collective-permute-start | bytes 196616 | tf_op jit(solution)/shard_map/ppermute | solution.py:635
  128.7 11.0 %collective-permute-start.24 = (bf16[64,512]{1,0:T(8,128)(2,1)S(1)}, bf16[64,512]{1,0:T(8,128)(2,1)S(1)}, u32[]{:S(2)}, u32[]{:S(2)}) collective-permute-start(bf16[64,512]{1,0:T(8,128)(2,1)S(1)} %get-tuple-element.221), channel_id=1, source_target_pairs={{0,64},{4,68},{8,72},{12,76},{16,80},{20,84},{24,88},{28,92},{32,9... | collective-permute-start | bytes 196616 | tf_op jit(solution)/shard_map/ppermute | solution.py:635
  130.5 9.3 %collective-permute-start.20 = (bf16[64,1536]{1,0:T(8,128)(2,1)S(1)}, bf16[64,1536]{1,0:T(8,128)(2,1)S(1)}, u32[]{:S(2)}, u32[]{:S(2)}) collective-permute-start(bf16[64,1536]{1,0:T(8,128)(2,1)S(1)} %pad_maximum_fusion.12), channel_id=1, source_target_pairs={{0,4},{4,8},{8,12},{12,0},{16,20},{20,24},{24,28},{28,16},{32,36},... | collective-permute-start | bytes 589832 | tf_op jit(solution)/shard_map/ppermute | solution.py:635
  139.7 7.2 %collective-permute-start.21 = (bf16[64,1536]{1,0:T(8,128)(2,1)S(1)}, bf16[64,1536]{1,0:T(8,128)(2,1)S(1)}, u32[]{:S(2)}, u32[]{:S(2)}) collective-permute-start(bf16[64,1536]{1,0:T(8,128)(2,1)S(1)} %pad_maximum_fusion.13), channel_id=1, source_target_pairs={{0,8},{4,12},{8,0},{12,4},{16,24},{20,28},{24,16},{28,20},{32,40},... | collective-permute-start | bytes 589832 | tf_op jit(solution)/shard_map/ppermute | solution.py:635
  139.7 7.2 %collective-permute-start.22 = (bf16[64,1536]{1,0:T(8,128)(2,1)S(1)}, bf16[64,1536]{1,0:T(8,128)(2,1)S(1)}, u32[]{:S(2)}, u32[]{:S(2)}) collective-permute-start(bf16[64,1536]{1,0:T(8,128)(2,1)S(1)} %pad_maximum_fusion.14), channel_id=1, source_target_pairs={{0,12},{4,0},{8,4},{12,8},{16,28},{20,16},{24,20},{28,24},{32,44},... | collective-permute-start | bytes 589832 | tf_op jit(solution)/shard_map/ppermute | solution.py:635
  139.7 8.3 %collective-permute-start.27 = (bf16[2,2,64,1024]{3,2,1,0:T(8,128)(2,1)S(1)}, bf16[2,2,64,1024]{3,2,1,0:T(8,128)(2,1)S(1)}, u32[]{:S(2)}, u32[]{:S(2)}) collective-permute-start(bf16[2,2,64,1024]{3,2,1,0:T(8,128)(2,1)S(1)} %get-tuple-element.179), channel_id=1, source_target_pairs={{0,2},{2,0},{1,3},{3,1},{4,6},{6,4},{5,7},{7,5},{8,10},{10,8},{9,1... | collective-permute-start | bytes 1572872 | tf_op jit(solution)/shard_map/ppermute | solution.py:597
  147.0 6.6 %collective-permute-start.26 = (bf16[32,2048]{1,0:T(8,128)(2,1)S(1)}, bf16[32,2048]{1,0:T(8,128)(2,1)S(1)}, u32[]{:S(2)}, u32[]{:S(2)}) collective-permute-start(bf16[32,2048]{1,0:T(8,128)(2,1)S(1)} %fusion), channel_id=1, source_target_pairs={{0,16},{4,20},{8,24},{12,28},{16,0},{20,4},{24,8},{28,12},{32,48},... | collective-permute-start | bytes 393224 | tf_op jit(solution)/shard_map/ppermute | solution.py:635
  (62 other events, 413.8 us)
where the time goes:
time: 160 us; the launch traced here: 159 us
  Pallas kernels  69.8 us (44%)
  waiting for transfers between devices  34.6 us (22%)
  starting transfers between devices  30.7 us (19%)
  local copies, waits for them, and re-layouts  17.6 us (11%)
  other arithmetic  4.68 us (3%)
  between operations  1.96 us (1%)
    pallas_call x3, Pallas kernels, attention(): pl.pallas_call(functools.partial(attention_kernel, quads), grid=(count,),...  29.9 us
    ppermute x19, waiting for transfers between devices, to_distance(): return lax.ppermute(value, 'lon', pairs)  24.8 us
    ppermute x19, starting transfers between devices, to_distance(): return lax.ppermute(value, 'lon', pairs)  22.2 us
    pallas_call x2, Pallas kernels, project(): pl.pallas_call(functools.partial(project_kernel, side), grid=(QUADS,), in...  18 us
    pallas_call x2, Pallas kernels, outputs(): pl.pallas_call(functools.partial(output_kernel, side), grid=(QUADS,), in_...  15.4 us
    unnamed x110, local copies, waits for them, and re-layouts  14.6 us
    ppermute x5, waiting for transfers between devices, swapped(): return lax.ppermute(value, axis, [(0, 1), (1, 0)])  9.06 us
    ppermute x1, starting transfers between devices, shifted_both(): return lax.ppermute(value, ('lon', 'lat'), pairs)  5.06 us
  transfers between devices with their start and end apart: 30, of which 12 were waited for; matrix products, arithmetic and copies ran while one was open for 3% of the time, Pallas kernels for 25%

commit v1 on v0

--- a/solution.py
+++ b/solution.py
@@ -45,6 +45,11 @@
 
 
 SCALARS = pl.BlockSpec(memory_space=pltpu.SMEM)
+IN_HBM = pl.BlockSpec(memory_space=pltpu.HBM)
+
+
+def in_hbm(a):
+    return pltpu.with_memory_space_constraint(a, pltpu.HBM)
 
 
 def dot(a, b):
@@ -187,27 +192,36 @@
     )(pick, f, g)
 
 
-def project_kernel(
-    side, pos_ref, own_ref, pick_ref, f_ref, g_ref, lon_ref, rim_ref, cor_ref, wq_ref, wk_ref, wv_ref, wo_ref,
-    xw_ref, gw_ref, nt_ref, q_ref, k_ref, v_ref, da_ref, nw,
-):
+def project_kernel(side, pos_ref, own_ref, pick_ref, f_ref, g_ref, wq_ref, wk_ref, wv_ref, wo_ref, rim_ref, *rest):
+    if side == 1:
+        lon_ref, cor_ref, rest = rest[0], rest[1], rest[2:]
+    xw_ref, gw_ref, nt_ref, q_ref, k_ref, v_ref, da_ref, nw, tokens, sems = rest
     samples, levels, _, width = f_ref.shape
+    kept = tokens.shape[3]
+    start = (SLON if side == 0 else SLON + SIDE) * ROWS
 
     @pl.when(pl.program_id(0) == 0)
     def _():
+        copies = [
+            pltpu.make_async_copy(ref.at[:, :, start : start + kept], tokens.at[arr], sems.at[arr])
+            for arr, ref in enumerate((f_ref, g_ref))
+        ]
+        for copy in copies:
+            copy.start()
+        for copy in copies:
+            copy.wait()
         for b in range(samples):
             got = []
-            for arr, ref in enumerate((f_ref, g_ref)):
+            for arr in range(2):
                 parts = []
                 for level in range(levels):
-                    if side == 0:
-                        parts.append(ref[b, level, SLON * ROWS : (SLON + SIDE) * ROWS])
-                    else:
-                        parts.append(ref[b, level, (SLON + SIDE) * ROWS :])
+                    parts.append(tokens[arr, b, level])
+                    if side == 1:
                         parts.append(lon_ref[arr, b, level])
-                own = jnp.concatenate(parts, axis=0)
-                rim = jnp.concatenate([rim_ref[arr, b], cor_ref[arr, b]], axis=0)
-                got.append((own, rim))
+                rim = rim_ref[arr, b]
+                if side == 1:
+                    rim = jnp.concatenate([rim, cor_ref[arr, b]], axis=0)
+                got.append((jnp.concatenate(parts, axis=0), rim))
             for wr in range(2):
                 at = slice((b * 2 + wr) * GROUP, (b * 2 + wr + 1) * GROUP)
                 x, g = (dot(own_ref[wr], own) for own, _ in got)
@@ -231,29 +245,27 @@
 
 
 def project(side, pos, f, g, lon_in, rim_in, cor_in, w_qkv, w_out):
-    width = f.shape[-1]
+    samples, levels, _, width = f.shape
     cols = width // QUADS
     whole = lambda n: (0, 0)
     full = lambda a: pl.BlockSpec(a.shape, lambda n: (0,) * a.ndim)
+    kept = (SIDE if side == 0 else SIDE - SLON) * ROWS
     own, pick = pick_own(), pick_rim(side)
+    if side == 0:
+        pick = pick[:, :RIM]
+    halos = (rim_in,) if side == 0 else (rim_in, lon_in, cor_in)
     tall = jax.ShapeDtypeStruct((HALF, width), BF)
     return pl.pallas_call(
         functools.partial(project_kernel, side),
         grid=(QUADS,),
-        in_specs=[
-            pl.BlockSpec(memory_space=pltpu.SMEM),
-            full(own),
-            full(pick),
-            full(f),
-            full(g),
-            full(lon_in),
-            full(rim_in),
-            full(cor_in),
+        in_specs=[SCALARS, full(own), full(pick), IN_HBM, IN_HBM]
+        + [
             pl.BlockSpec((width, cols), lambda n: (0, n)),
             pl.BlockSpec((width, cols), lambda n: (0, QUADS + n)),
             pl.BlockSpec((width, cols), lambda n: (0, 2 * QUADS + n)),
             pl.BlockSpec((cols, width), lambda n: (n, 0)),
-        ],
+        ]
+        + [full(a) for a in halos],
         out_specs=[
             pl.BlockSpec((HALF, width), whole),
             pl.BlockSpec((HALF, width), whole),
@@ -261,15 +273,29 @@
         ]
         + [pl.BlockSpec((HALF, cols), lambda n: (0, n))] * 4,
         out_shape=[pltpu.HBM((HALF, width), BF), tall, jax.ShapeDtypeStruct((width, HALF), BF)] + [tall] * 4,
-        scratch_shapes=[pltpu.VMEM((HALF, width), BF)],
+        scratch_shapes=[
+            pltpu.VMEM((HALF, width), BF),
+            pltpu.VMEM((2, samples, levels, kept, width), BF),
+            pltpu.SemaphoreType.DMA((2,)),
+        ],
         compiler_params=params(20),
         cost_estimate=cost(9),
         name="project",
-    )(pos, own, pick, f, g, lon_in, rim_in, cor_in, w_qkv, w_qkv, w_qkv, w_out)
+    )(pos, own, pick, in_hbm(f), in_hbm(g), w_qkv, w_qkv, w_qkv, w_out, *halos)
 
 
 def attention_kernel(quads, pos_ref, bias_ref, *rest):
-    sides, rest = (rest[:6], rest[6:12]), rest[12:]
+    sides, rest = [rest[:6], rest[6:12]], rest[12:]
+    copies = []
+    if len(quads) == 1:
+        *rest, part, sems = rest
+        at = slice(quads[0] * (part.shape[2]), (quads[0] + 1) * part.shape[2])
+        copies = [
+            pltpu.make_async_copy(sides[1][2 + i].at[:, at], part.at[i], sems.at[i]) for i in range(4)
+        ]
+        sides[1] = (*sides[1][:2], *(part.at[i] for i in range(4)))
+        for copy in copies:
+            copy.start()
     if quads == (3,):
         kin_ref, rest = rest[0], rest[1:]
     if quads == (1,):
@@ -339,6 +365,9 @@
 
     def units(src, dst):
         for side in range(2):
+            if side == 1:
+                for copy in copies:
+                    copy.wait()
 
             def sample(b, carry):
                 works = [
@@ -431,10 +460,15 @@
     whole = lambda n: (0, 0)
     in_specs = [SCALARS, pl.BlockSpec(bias.shape, lambda n: (0, 0, 0))]
     operands = [pos, bias]
-    for _, gw, nt, q, k, v, da in sides:
+    for side, (_, gw, nt, *columns) in enumerate(sides):
         in_specs += [pl.BlockSpec((width, HALF), whole), pl.BlockSpec((HALF, width), whole)]
-        in_specs += [pl.BlockSpec((HALF, cols), lambda n: (0, quad(n)))] * 4
-        operands += [nt, gw, q, k, v, da]
+        operands += [nt, gw]
+        if count == 1 and side == 1:
+            in_specs += [IN_HBM] * 4
+            operands += [in_hbm(a) for a in columns]
+        else:
+            in_specs += [pl.BlockSpec((HALF, cols), lambda n: (0, quad(n)))] * 4
+            operands += columns
     if before is not None:
         in_specs.append(pl.BlockSpec((width, cols), whole))
         operands.append(before)
@@ -455,7 +489,8 @@
         in_specs=in_specs,
         out_specs=out_specs,
         out_shape=[pltpu.HBM(s, BF) if n < 4 and count == 2 else jax.ShapeDtypeStruct(s, BF) for n, s in enumerate(shapes)],
-        scratch_shapes=[pltpu.VMEM((cols, 2 * HALF), BF)],
+        scratch_shapes=[pltpu.VMEM((cols, 2 * HALF), BF)]
+        + ([pltpu.VMEM((4, HALF, cols), BF), pltpu.SemaphoreType.DMA((4,))] if count == 1 else []),
         compiler_params=params(20),
         cost_estimate=cost(11 * count),
         name="attention",

time: 160 us -> 153 us (0.956)
  local copies, waits for them, and re-layouts: 17.6 us -> 7.58 us
  Pallas kernels: 69.8 us -> 73.7 us
    unnamed x110 -> x86, local copies, waits for them, and re-layouts: 14.6 us -> 4.64 us
    pallas_call x2, Pallas kernels: 18 us -> 21.7 us  [project(): pl.pallas_call(functools.partial(project_kernel, side), grid=(QUADS,), in...]
  transfers between devices with their start and end apart: 30 -> 30, of which waited for: 12 -> 13; matrix products, arithmetic and copies ran while one was open for 3% -> 3% of each run, Pallas kernels for 25% -> 28%
where the time goes in v1:
time: 153 us
  Pallas kernels  73.7 us (48%)
  waiting for transfers between devices  34.5 us (23%)
  starting transfers between devices  30.7 us (20%)
  local copies, waits for them, and re-layouts  7.58 us (5%)
  other arithmetic  4.73 us (3%)
  between operations  1.89 us (1%)
    pallas_call x3, Pallas kernels, attention(): pl.pallas_call(functools.partial(attention_kernel, quads), grid=(count,),...  30 us
    ppermute x19, waiting for transfers between devices, to_distance(): return lax.ppermute(value, 'lon', pairs)  24.7 us
    ppermute x19, starting transfers between devices, to_distance(): return lax.ppermute(value, 'lon', pairs)  22.2 us
    pallas_call x2, Pallas kernels, project(): pl.pallas_call(functools.partial(project_kernel, side), grid=(QUADS,), in...  21.7 us
    pallas_call x2, Pallas kernels, outputs(): pl.pallas_call(functools.partial(output_kernel, side), grid=(QUADS,), in_...  15.5 us
    ppermute x5, waiting for transfers between devices, swapped(): return lax.ppermute(value, axis, [(0, 1), (1, 0)])  9.03 us
    ppermute x1, starting transfers between devices, shifted_both(): return lax.ppermute(value, ('lon', 'lat'), pairs)  5.06 us
    unnamed x86, local copies, waits for them, and re-layouts  4.64 us
  transfers between devices with their start and end apart: 30, of which 13 were waited for; matrix products, arithmetic and copies ran while one was open for 3% of the time, Pallas kernels for 28%

profile of v1, /device:TPU:64, one launch (start us, length us, event | category | flops | bytes accessed | tf_op | source)
XLA Modules:
  0.0 153.1 jit_solution(18142405528756885610)
XLA Ops:
  0.7 3.6 %strips.1 = (bf16[2,2,3,16,1024]{4,3,2,1,0:T(8,128)(2,1)}, bf16[2,2,128,1024]{3,2,1,0:T(8,128)(2,1)}, bf16[2,2,16,1024]{3,2,1,0:T(8,128)(2,1)}) custom-call(bf16[144,480]{1,0:T(8,128)(2,1)} %constant.132.clone.pick_ref, bf16[2,3,160,1024]{3,2,1,0:T(8,128)(2,1)} %bitcast.60, bf16[2,3,160,1024]{3,2,1,0:T(8,128)(2,1)} %bitcast.63), custom_call_target="tpu_custom_call" | custom-call | flops 3300000000 | bytes 1000000 | tf_op jit(solution)/shard_map/strips/pallas_call | solution.py:181
  4.3 5.1 %collective-permute-start.2 = (bf16[2,2,16,1024]{3,2,1,0:T(8,128)(2,1)}, bf16[2,2,16,1024]{3,2,1,0:T(8,128)(2,1)S(1)}, u32[]{:S(2)}, u32[]{:S(2)}) collective-permute-start(bf16[2,2,16,1024]{3,2,1,0:T(8,128)(2,1)} %get-tuple-element.103), channel_id=1, source_target_pairs={{0,126},{2,124},{4,2},{6,0},{8,6},{10,4},{12,10},{14,8},{16,14},{1... | collective-permute-start | bytes 393224 | tf_op jit(solution)/shard_map/ppermute | solution.py:642
  10.8 2.8 %copy-done = bf16[1024,3072]{1,0:T(8,128)(2,1)S(1)} copy-done((bf16[1024,3072]{1,0:T(8,128)(2,1)S(1)}, bf16[1024,3072]{1,0:T(8,128)(2,1)}, u32[]{:S(2)}) %copy-start) | copy-done | bytes 6291480
  15.3 10.4 %project.2 = (bf16[512,1024]{1,0:T(8,128)(2,1)}, bf16[512,1024]{1,0:T(8,128)(2,1)S(1)}, bf16[1024,512]{1,0:T(8,128)(2,1)S(1)}, bf16[512,1024]{1,0:T(8,128)(2,1)S...) custom-call(s32[2]{0:T(128)S(1)} %pad_add_fusion.1.pos_ref, ...), custom_call_target="tpu_custom_call" | custom-call | flops 9900000256 | bytes 1000000 | tf_op jit(solution)/shard_map/project/pallas_call | solution.py:258
  25.8 11.3 %project.3 = (bf16[512,1024]{1,0:T(8,128)(2,1)}, bf16[512,1024]{1,0:T(8,128)(2,1)S(1)}, bf16[1024,512]{1,0:T(8,128)(2,1)S(1)}, bf16[512,1024]{1,0:T(8,128)(2,1)S...) custom-call(s32[2]{0:T(128)S(1)} %pad_add_fusion.1.pos_ref, ...), custom_call_target="tpu_custom_call" | custom-call | flops 9900000256 | bytes 1000000 | tf_op jit(solution)/shard_map/project/pallas_call | solution.py:258
  37.2 15.9 %attention.3 = (bf16[1024,512]{1,0:T(8,128)(2,1)}, bf16[1024,512]{1,0:T(8,128)(2,1)}, bf16[1024,512]{1,0:T(8,128)(2,1)}, bf16[1024,512]{1,0:T(8,128)(2,1)}, bf16...) custom-call(s32[2]{0:T(128)S(1)} %pad_add_fusion.1.pos_ref, ...), custom_call_target="tpu_custom_call" | custom-call | flops 24199999488 | bytes 1000000 | tf_op jit(solution)/shard_map/attention/pallas_call | solution.py:486
  53.7 3.2 %collective-permute-done.3 = bf16[1024,768]{1,0:T(8,128)(2,1)} collective-permute-done((bf16[1024,768]{1,0:T(8,128)(2,1)}, bf16[1024,768]{1,0:T(8,128)(2,1)}, u32[]{:S(2)}, u32[]{:S(2)}) %collective-permute-start.3) | collective-permute-done | bytes 1572896 | tf_op jit(solution)/shard_map/ppermute | solution.py:662
  57.0 1.9 %add_convert_fusion = bf16[1024,768]{1,0:T(8,128)(2,1)S(1)} fusion(bf16[1024,768]{1,0:T(8,128)(2,1)} %collective-permute-done.3, bf16[1024,768]{1,0:T(8,128)(2,1)S(1)} %get-tuple-element.110), kind=kLoop, calls=%fused_computation | loop fusion | flops 3145728 | bytes 4718592 | tf_op jit(solution)/shard_map/convert_element_type | solution.py:702
  61.5 7.1 %attention.4 = (bf16[1024,256]{1,0:T(8,128)(2,1)S(1)}, bf16[1024,256]{1,0:T(8,128)(2,1)S(1)}, bf16[1024,256]{1,0:T(8,128)(2,1)S(1)}, bf16[1024,256]{1,0:T(8,128)...) custom-call(s32[2]{0:T(128)S(1)} %pad_add_fusion.1.pos_ref, ...), custom_call_target="tpu_custom_call" | custom-call | flops 12099999744 | bytes 1000000 | tf_op jit(solution)/shard_map/attention/pallas_call | solution.py:486
  68.8 3.2 %collective-permute-start.6 = (bf16[256,768]{1,0:T(8,128)(2,1)S(1)}, bf16[256,768]{1,0:T(8,128)(2,1)S(1)}, u32[]{:S(2)}, u32[]{:S(2)}) collective-permute-start(bf16[256,768]{1,0:T(8,128)(2,1)S(1)} %pad_maximum_fusion.1), channel_id=1, source_target_pairs={{0,32},{4,36},{8,40},{12,44},{16,48},{20,52},{24,56},{28,60},{32,6... | collective-permute-start | bytes 1179656 | tf_op jit(solution)/shard_map/ppermute | solution.py:670
  72.0 7.1 %attention.5 = (bf16[1024,256]{1,0:T(8,128)(2,1)S(1)}, bf16[1024,256]{1,0:T(8,128)(2,1)S(1)}, bf16[1024,256]{1,0:T(8,128)(2,1)S(1)}, bf16[1024,256]{1,0:T(8,128)...) custom-call(s32[2]{0:T(128)S(1)} %pad_add_fusion.1.pos_ref, ...), custom_call_target="tpu_custom_call" | custom-call | flops 12099999744 | bytes 1000000 | tf_op jit(solution)/shard_map/attention/pallas_call | solution.py:486
  80.1 2.2 %collective-permute-done.7 = bf16[256,768]{1,0:T(8,128)(2,1)S(1)} collective-permute-done((bf16[256,768]{1,0:T(8,128)(2,1)S(1)}, bf16[256,768]{1,0:T(8,128)(2,1)S(1)}, u32[]{:S(2)}, u32[]{:S(2)}) %collective-permute-start.7) | collective-permute-done | bytes 393248 | tf_op jit(solution)/shard_map/ppermute | solution.py:670
  87.9 2.0 %collective-permute-start.11 = (bf16[128,512]{1,0:T(8,128)(2,1)S(1)}, bf16[128,512]{1,0:T(8,128)(2,1)S(1)}, u32[]{:S(2)}, u32[]{:S(2)}) collective-permute-start(bf16[128,512]{1,0:T(8,128)(2,1)S(1)} %get-tuple-element.223), channel_id=1, source_target_pairs={{0,4},{4,8},{8,12},{12,0},{16,20},{20,24},{24,28},{28,16},{32,36},... | collective-permute-start | bytes 393224 | tf_op jit(solution)/shard_map/ppermute | solution.py:670
  90.3 3.0 %collective-permute-start.13 = (bf16[128,768]{1,0:T(8,128)(2,1)S(1)}, bf16[128,768]{1,0:T(8,128)(2,1)S(1)}, u32[]{:S(2)}, u32[]{:S(2)}) collective-permute-start(bf16[128,768]{1,0:T(8,128)(2,1)S(1)} %get-tuple-element.216), channel_id=1, source_target_pairs={{0,32},{4,36},{8,40},{12,44},{16,48},{20,52},{24,56},{28,60},{32,6... | collective-permute-start | bytes 589832 | tf_op jit(solution)/shard_map/ppermute | solution.py:670
  93.3 7.8 %outputs.2 = (bf16[2,3,64,1024]{3,2,1,0:T(8,128)(2,1)S(1)}, bf16[2,3,64,1024]{3,2,1,0:T(8,128)(2,1)S(1)}, bf16[2,2,64,1024]{3,2,1,0:T(8,128)(2,1)S(1)}, bf16[2,2,3,16,1024]{4,3,2,1,0:T(8,128)(2,1)S(1)}) custom-call(bf16[240,256]{1,0:T(8,128)(2,1)S(1)} %copy-done.5, bf16[64,128]{1,0:T(8,128)(2,1)S(1)} %copy-done.10, bf16[512,1024]{1,0:T(8,128)(2,1)S(1)} %copy-done.12, ...), custom_call_target="tpu_custom_call" | custom-call | flops 8800000000 | bytes 1000000 | tf_op jit(solution)/shard_map/outputs/pallas_call | solution.py:557
  104.8 2.0 %collective-permute-start.17 = (bf16[256,512]{1,0:T(8,128)(2,1)S(1)}, bf16[256,512]{1,0:T(8,128)(2,1)S(1)}, u32[]{:S(2)}, u32[]{:S(2)}) collective-permute-start(bf16[256,512]{1,0:T(8,128)(2,1)S(1)} %pad_maximum_fusion.11), channel_id=1, source_target_pairs={{0,12},{4,0},{8,4},{12,8},{16,28},{20,16},{24,20},{28,24},{32,44},... | collective-permute-start | bytes 786440 | tf_op jit(solution)/shard_map/ppermute | solution.py:670
  106.8 2.9 %collective-permute-start.18 = (bf16[256,768]{1,0:T(8,128)(2,1)S(1)}, bf16[256,768]{1,0:T(8,128)(2,1)S(1)}, u32[]{:S(2)}, u32[]{:S(2)}) collective-permute-start(bf16[256,768]{1,0:T(8,128)(2,1)S(1)} %pad_maximum_fusion.7), channel_id=1, source_target_pairs={{0,32},{4,36},{8,40},{12,44},{16,48},{20,52},{24,56},{28,60},{32,6... | collective-permute-start | bytes 1179656 | tf_op jit(solution)/shard_map/ppermute | solution.py:670
  109.7 7.8 %outputs.3 = (bf16[2,3,80,1024]{3,2,1,0:T(8,128)(2,1)S(1)}, bf16[2,3,80,1024]{3,2,1,0:T(8,128)(2,1)S(1)}, bf16[2,2,64,1024]{3,2,1,0:T(8,128)(2,1)S(1)}) custom-call(bf16[240,256]{1,0:T(8,128)(2,1)S(1)} %copy-done.5, bf16[64,128]{1,0:T(8,128)(2,1)S(1)} %copy-done.10, bf16[512,1024]{1,0:T(8,128)(2,1)S(1)} %copy-done.21, bf16[512,1024]{1,0:T(8,128)(2,1)S(1)} %copy-done.23, ...), custom_call_target="tpu_custom_call" | custom-call | flops 8800000000 | bytes 1000000 | tf_op jit(solution)/shard_map/outputs/pallas_call | solution.py:557
  117.9 2.2 %collective-permute-done.19 = bf16[256,768]{1,0:T(8,128)(2,1)S(1)} collective-permute-done((bf16[256,768]{1,0:T(8,128)(2,1)S(1)}, bf16[256,768]{1,0:T(8,128)(2,1)S(1)}, u32[]{:S(2)}, u32[]{:S(2)}) %collective-permute-start.19) | collective-permute-done | bytes 393248 | tf_op jit(solution)/shard_map/ppermute | solution.py:670
  124.5 9.1 %collective-permute-done.23 = bf16[64,512]{1,0:T(8,128)(2,1)S(1)} collective-permute-done((bf16[64,512]{1,0:T(8,128)(2,1)S(1)}, bf16[64,512]{1,0:T(8,128)(2,1)S(1)}, u32[]{:S(2)}, u32[]{:S(2)}) %collective-permute-start.23) | collective-permute-done | bytes 65568 | tf_op jit(solution)/shard_map/ppermute | solution.py:670
  135.4 5.3 %collective-permute-done.21 = bf16[64,1536]{1,0:T(8,128)(2,1)S(1)} collective-permute-done((bf16[64,1536]{1,0:T(8,128)(2,1)S(1)}, bf16[64,1536]{1,0:T(8,128)(2,1)S(1)}, u32[]{:S(2)}, u32[]{:S(2)}) %collective-permute-start.21) | collective-permute-done | bytes 196640 | tf_op jit(solution)/shard_map/ppermute | solution.py:670
  141.9 2.6 %merge.1 = (bf16[2,3,160,1024]{3,2,1,0:T(8,128)(2,1)}, bf16[2,3,160,1024]{3,2,1,0:T(8,128)(2,1)}) custom-call(bf16[3,80,64]{2,1,0:T(8,128)(2,1)S(1)} %copy-done.7, bf16[3,64,64]{2,1,0:T(8,128)(2,1)S(1)} %copy-done.8, bf16[2,3,80,1024]{3,2,1,0:T(8,128)(2,1)S(1)} %get-tuple-element.175.y0, bf16[2,3,80,1024]{3,2,1,0:T(8,128)(2,1)S(1)} %get-tuple-element.176.g0, ...), custom_call_target="tpu_custom_call" | custom-call | flops 4400000000 | bytes 1000000 | tf_op jit(solution)/shard_map/merge/pallas_call | solution.py:615
  144.5 2.9 %collective-permute-done.26 = bf16[32,2048]{1,0:T(8,128)(2,1)S(1)} collective-permute-done((bf16[32,2048]{1,0:T(8,128)(2,1)S(1)}, bf16[32,2048]{1,0:T(8,128)(2,1)S(1)}, u32[]{:S(2)}, u32[]{:S(2)}) %collective-permute-start.26) | collective-permute-done | bytes 131104 | tf_op jit(solution)/shard_map/ppermute | solution.py:670
  148.9 3.0 %collective-permute-done.29 = bf16[32,1024]{1,0:T(8,128)(2,1)S(1)} collective-permute-done((bf16[32,1024]{1,0:T(8,128)(2,1)S(1)}, bf16[32,1024]{1,0:T(8,128)(2,1)S(1)}, u32[]{:S(2)}, u32[]{:S(2)}) %collective-permute-start.29) | collective-permute-done | bytes 65568 | tf_op jit(solution)/shard_map/ppermute | solution.py:662
  (202 shorter events, 26.9 us)
Async XLA Ops:
  4.3 21.5 %collective-permute-start.2 = (bf16[2,2,16,1024]{3,2,1,0:T(8,128)(2,1)}, bf16[2,2,16,1024]{3,2,1,0:T(8,128)(2,1)S(1)}, u32[]{:S(2)}, u32[]{:S(2)}) collective-permute-start(bf16[2,2,16,1024]{3,2,1,0:T(8,128)(2,1)} %get-tuple-element.103), channel_id=1, source_target_pairs={{0,126},{2,124},{4,2},{6,0},{8,6},{10,4},{12,10},{14,8},{16,14},{1... | collective-permute-start | bytes 393224 | tf_op jit(solution)/shard_map/ppermute | solution.py:642
  9.4 16.4 %collective-permute-start.1 = (bf16[2,2,3,16,1024]{4,3,2,1,0:T(8,128)(2,1)}, bf16[2,2,3,16,1024]{4,3,2,1,0:T(8,128)(2,1)}, u32[]{:S(2)}, u32[]{:S(2)}) collective-permute-start(bf16[2,2,3,16,1024]{4,3,2,1,0:T(8,128)(2,1)} %get-tuple-element.102), channel_id=1, source_target_pairs={{0,124},{4,0},{8,4},{12,8},{16,12},{20,16},{24,20},{28,24},{32,28}... | collective-permute-start | bytes 1179656 | tf_op jit(solution)/shard_map/ppermute | solution.py:632
  53.4 29.0 %collective-permute-start.10 = (bf16[512,512]{1,0:T(8,128)(2,1)S(1)}, bf16[512,512]{1,0:T(8,128)(2,1)S(1)}, u32[]{:S(2)}, u32[]{:S(2)}) collective-permute-start(bf16[512,512]{1,0:T(8,128)(2,1)S(1)} %get-tuple-element.134), channel_id=1, source_target_pairs={{0,2},{2,0},{1,3},{3,1},{4,6},{6,4},{5,7},{7,5},{8,10},{10,8},{9,1... | collective-permute-start | bytes 1572872 | tf_op jit(solution)/shard_map/ppermute | solution.py:662
  59.1 9.4 %collective-permute-start.5 = (bf16[128,768]{1,0:T(8,128)(2,1)S(1)}, bf16[128,768]{1,0:T(8,128)(2,1)S(1)}, u32[]{:S(2)}, u32[]{:S(2)}) collective-permute-start(bf16[128,768]{1,0:T(8,128)(2,1)S(1)} %get-tuple-element.217), channel_id=1, source_target_pairs={{0,96},{4,100},{8,104},{12,108},{16,112},{20,116},{24,120},{28,124... | collective-permute-start | bytes 589832 | tf_op jit(solution)/shard_map/ppermute | solution.py:670
  59.5 9.1 %collective-permute-start.4 = (bf16[128,768]{1,0:T(8,128)(2,1)S(1)}, bf16[128,768]{1,0:T(8,128)(2,1)S(1)}, u32[]{:S(2)}, u32[]{:S(2)}) collective-permute-start(bf16[128,768]{1,0:T(8,128)(2,1)S(1)} %get-tuple-element.218), channel_id=1, source_target_pairs={{0,32},{4,36},{8,40},{12,44},{16,48},{20,52},{24,56},{28,60},{32,6... | collective-permute-start | bytes 589832 | tf_op jit(solution)/shard_map/ppermute | solution.py:670
  68.8 11.3 %collective-permute-start.6 = (bf16[256,768]{1,0:T(8,128)(2,1)S(1)}, bf16[256,768]{1,0:T(8,128)(2,1)S(1)}, u32[]{:S(2)}, u32[]{:S(2)}) collective-permute-start(bf16[256,768]{1,0:T(8,128)(2,1)S(1)} %pad_maximum_fusion.1), channel_id=1, source_target_pairs={{0,32},{4,36},{8,40},{12,44},{16,48},{20,52},{24,56},{28,60},{32,6... | collective-permute-start | bytes 1179656 | tf_op jit(solution)/shard_map/ppermute | solution.py:670
  72.0 10.3 %collective-permute-start.7 = (bf16[256,768]{1,0:T(8,128)(2,1)S(1)}, bf16[256,768]{1,0:T(8,128)(2,1)S(1)}, u32[]{:S(2)}, u32[]{:S(2)}) collective-permute-start(bf16[256,768]{1,0:T(8,128)(2,1)S(1)} %pad_maximum_fusion.2), channel_id=1, source_target_pairs={{0,96},{4,100},{8,104},{12,108},{16,112},{20,116},{24,120},{28,124... | collective-permute-start | bytes 1179656 | tf_op jit(solution)/shard_map/ppermute | solution.py:670
  87.8 13.5 %collective-permute-start.12 = (bf16[128,512]{1,0:T(8,128)(2,1)S(1)}, bf16[128,512]{1,0:T(8,128)(2,1)S(1)}, u32[]{:S(2)}, u32[]{:S(2)}) collective-permute-start(bf16[128,512]{1,0:T(8,128)(2,1)S(1)} %get-tuple-element.222), channel_id=1, source_target_pairs={{0,12},{4,0},{8,4},{12,8},{16,28},{20,16},{24,20},{28,24},{32,44},... | collective-permute-start | bytes 393224 | tf_op jit(solution)/shard_map/ppermute | solution.py:670
  87.9 13.4 %collective-permute-start.11 = (bf16[128,512]{1,0:T(8,128)(2,1)S(1)}, bf16[128,512]{1,0:T(8,128)(2,1)S(1)}, u32[]{:S(2)}, u32[]{:S(2)}) collective-permute-start(bf16[128,512]{1,0:T(8,128)(2,1)S(1)} %get-tuple-element.223), channel_id=1, source_target_pairs={{0,4},{4,8},{8,12},{12,0},{16,20},{20,24},{24,28},{28,16},{32,36},... | collective-permute-start | bytes 393224 | tf_op jit(solution)/shard_map/ppermute | solution.py:670
  89.9 11.4 %collective-permute-start.14 = (bf16[128,768]{1,0:T(8,128)(2,1)S(1)}, bf16[128,768]{1,0:T(8,128)(2,1)S(1)}, u32[]{:S(2)}, u32[]{:S(2)}) collective-permute-start(bf16[128,768]{1,0:T(8,128)(2,1)S(1)} %get-tuple-element.215), channel_id=1, source_target_pairs={{0,96},{4,100},{8,104},{12,108},{16,112},{20,116},{24,120},{28,124... | collective-permute-start | bytes 589832 | tf_op jit(solution)/shard_map/ppermute | solution.py:670
  90.3 11.1 %collective-permute-start.13 = (bf16[128,768]{1,0:T(8,128)(2,1)S(1)}, bf16[128,768]{1,0:T(8,128)(2,1)S(1)}, u32[]{:S(2)}, u32[]{:S(2)}) collective-permute-start(bf16[128,768]{1,0:T(8,128)(2,1)S(1)} %get-tuple-element.216), channel_id=1, source_target_pairs={{0,32},{4,36},{8,40},{12,44},{16,48},{20,52},{24,56},{28,60},{32,6... | collective-permute-start | bytes 589832 | tf_op jit(solution)/shard_map/ppermute | solution.py:670
  103.5 14.1 %collective-permute-start.16 = (bf16[256,512]{1,0:T(8,128)(2,1)S(1)}, bf16[256,512]{1,0:T(8,128)(2,1)S(1)}, u32[]{:S(2)}, u32[]{:S(2)}) collective-permute-start(bf16[256,512]{1,0:T(8,128)(2,1)S(1)} %pad_maximum_fusion.10), channel_id=1, source_target_pairs={{0,4},{4,8},{8,12},{12,0},{16,20},{20,24},{24,28},{28,16},{32,36},... | collective-permute-start | bytes 786440 | tf_op jit(solution)/shard_map/ppermute | solution.py:670
  104.8 12.8 %collective-permute-start.17 = (bf16[256,512]{1,0:T(8,128)(2,1)S(1)}, bf16[256,512]{1,0:T(8,128)(2,1)S(1)}, u32[]{:S(2)}, u32[]{:S(2)}) collective-permute-start(bf16[256,512]{1,0:T(8,128)(2,1)S(1)} %pad_maximum_fusion.11), channel_id=1, source_target_pairs={{0,12},{4,0},{8,4},{12,8},{16,28},{20,16},{24,20},{28,24},{32,44},... | collective-permute-start | bytes 786440 | tf_op jit(solution)/shard_map/ppermute | solution.py:670
  106.8 11.0 %collective-permute-start.18 = (bf16[256,768]{1,0:T(8,128)(2,1)S(1)}, bf16[256,768]{1,0:T(8,128)(2,1)S(1)}, u32[]{:S(2)}, u32[]{:S(2)}) collective-permute-start(bf16[256,768]{1,0:T(8,128)(2,1)S(1)} %pad_maximum_fusion.7), channel_id=1, source_target_pairs={{0,32},{4,36},{8,40},{12,44},{16,48},{20,52},{24,56},{28,60},{32,6... | collective-permute-start | bytes 1179656 | tf_op jit(solution)/shard_map/ppermute | solution.py:670
  109.7 10.3 %collective-permute-start.19 = (bf16[256,768]{1,0:T(8,128)(2,1)S(1)}, bf16[256,768]{1,0:T(8,128)(2,1)S(1)}, u32[]{:S(2)}, u32[]{:S(2)}) collective-permute-start(bf16[256,768]{1,0:T(8,128)(2,1)S(1)} %pad_maximum_fusion.8), channel_id=1, source_target_pairs={{0,96},{4,100},{8,104},{12,108},{16,112},{20,116},{24,120},{28,124... | collective-permute-start | bytes 1179656 | tf_op jit(solution)/shard_map/ppermute | solution.py:670
  117.5 24.4 %collective-permute-start.28 = (bf16[2,2,3,16,1024]{4,3,2,1,0:T(8,128)(2,1)S(1)}, bf16[2,2,3,16,1024]{4,3,2,1,0:T(8,128)(2,1)S(1)}, u32[]{:S(2)}, u32[]{:S(2)}) collective-permute-start(bf16[2,2,3,16,1024]{4,3,2,1,0:T(8,128)(2,1)S(1)} %patch.1), channel_id=1, source_target_pairs={{0,4},{4,8},{8,12},{12,16},{16,20},{20,24},{24,28},{28,32},{32,36}... | collective-permute-start | bytes 1179656 | tf_op jit(solution)/shard_map/ppermute | solution.py:632
  120.4 13.1 %collective-permute-start.23 = (bf16[64,512]{1,0:T(8,128)(2,1)S(1)}, bf16[64,512]{1,0:T(8,128)(2,1)S(1)}, u32[]{:S(2)}, u32[]{:S(2)}) collective-permute-start(bf16[64,512]{1,0:T(8,128)(2,1)S(1)} %get-tuple-element.219), channel_id=1, source_target_pairs={{0,32},{4,36},{8,40},{12,44},{16,48},{20,52},{24,56},{28,60},{32,6... | collective-permute-start | bytes 196616 | tf_op jit(solution)/shard_map/ppermute | solution.py:670
  122.0 11.6 %collective-permute-start.25 = (bf16[64,512]{1,0:T(8,128)(2,1)S(1)}, bf16[64,512]{1,0:T(8,128)(2,1)S(1)}, u32[]{:S(2)}, u32[]{:S(2)}) collective-permute-start(bf16[64,512]{1,0:T(8,128)(2,1)S(1)} %get-tuple-element.220), channel_id=1, source_target_pairs={{0,96},{4,100},{8,104},{12,108},{16,112},{20,116},{24,120},{28,124... | collective-permute-start | bytes 196616 | tf_op jit(solution)/shard_map/ppermute | solution.py:670
  122.5 11.1 %collective-permute-start.24 = (bf16[64,512]{1,0:T(8,128)(2,1)S(1)}, bf16[64,512]{1,0:T(8,128)(2,1)S(1)}, u32[]{:S(2)}, u32[]{:S(2)}) collective-permute-start(bf16[64,512]{1,0:T(8,128)(2,1)S(1)} %get-tuple-element.221), channel_id=1, source_target_pairs={{0,64},{4,68},{8,72},{12,76},{16,80},{20,84},{24,88},{28,92},{32,9... | collective-permute-start | bytes 196616 | tf_op jit(solution)/shard_map/ppermute | solution.py:670
  124.3 11.1 %collective-permute-start.20 = (bf16[64,1536]{1,0:T(8,128)(2,1)S(1)}, bf16[64,1536]{1,0:T(8,128)(2,1)S(1)}, u32[]{:S(2)}, u32[]{:S(2)}) collective-permute-start(bf16[64,1536]{1,0:T(8,128)(2,1)S(1)} %pad_maximum_fusion.12), channel_id=1, source_target_pairs={{0,4},{4,8},{8,12},{12,0},{16,20},{20,24},{24,28},{28,16},{32,36},... | collective-permute-start | bytes 589832 | tf_op jit(solution)/shard_map/ppermute | solution.py:670
  133.5 7.2 %collective-permute-start.21 = (bf16[64,1536]{1,0:T(8,128)(2,1)S(1)}, bf16[64,1536]{1,0:T(8,128)(2,1)S(1)}, u32[]{:S(2)}, u32[]{:S(2)}) collective-permute-start(bf16[64,1536]{1,0:T(8,128)(2,1)S(1)} %pad_maximum_fusion.13), channel_id=1, source_target_pairs={{0,8},{4,12},{8,0},{12,4},{16,24},{20,28},{24,16},{28,20},{32,40},... | collective-permute-start | bytes 589832 | tf_op jit(solution)/shard_map/ppermute | solution.py:670
  133.5 7.2 %collective-permute-start.22 = (bf16[64,1536]{1,0:T(8,128)(2,1)S(1)}, bf16[64,1536]{1,0:T(8,128)(2,1)S(1)}, u32[]{:S(2)}, u32[]{:S(2)}) collective-permute-start(bf16[64,1536]{1,0:T(8,128)(2,1)S(1)} %pad_maximum_fusion.14), channel_id=1, source_target_pairs={{0,12},{4,0},{8,4},{12,8},{16,28},{20,16},{24,20},{28,24},{32,44},... | collective-permute-start | bytes 589832 | tf_op jit(solution)/shard_map/ppermute | solution.py:670
  133.6 8.3 %collective-permute-start.27 = (bf16[2,2,64,1024]{3,2,1,0:T(8,128)(2,1)S(1)}, bf16[2,2,64,1024]{3,2,1,0:T(8,128)(2,1)S(1)}, u32[]{:S(2)}, u32[]{:S(2)}) collective-permute-start(bf16[2,2,64,1024]{3,2,1,0:T(8,128)(2,1)S(1)} %get-tuple-element.179), channel_id=1, source_target_pairs={{0,2},{2,0},{1,3},{3,1},{4,6},{6,4},{5,7},{7,5},{8,10},{10,8},{9,1... | collective-permute-start | bytes 1572872 | tf_op jit(solution)/shard_map/ppermute | solution.py:632
  140.8 6.6 %collective-permute-start.26 = (bf16[32,2048]{1,0:T(8,128)(2,1)S(1)}, bf16[32,2048]{1,0:T(8,128)(2,1)S(1)}, u32[]{:S(2)}, u32[]{:S(2)}) collective-permute-start(bf16[32,2048]{1,0:T(8,128)(2,1)S(1)} %fusion), channel_id=1, source_target_pairs={{0,16},{4,20},{8,24},{12,28},{16,0},{20,4},{24,8},{28,12},{32,48},... | collective-permute-start | bytes 393224 | tf_op jit(solution)/shard_map/ppermute | solution.py:670
  (50 other events, 398.0 us)

commit v2 on v1

--- a/solution.py
+++ b/solution.py
@@ -197,7 +197,7 @@
         lon_ref, cor_ref, rest = rest[0], rest[1], rest[2:]
     xw_ref, gw_ref, nt_ref, q_ref, k_ref, v_ref, da_ref, nw, tokens, sems = rest
     samples, levels, _, width = f_ref.shape
-    kept = tokens.shape[3]
+    kept = (SIDE if side == 0 else SIDE - SLON) * ROWS
     start = (SLON if side == 0 else SLON + SIDE) * ROWS
 
     @pl.when(pl.program_id(0) == 0)
@@ -205,6 +205,7 @@
         copies = [
             pltpu.make_async_copy(ref.at[:, :, start : start + kept], tokens.at[arr], sems.at[arr])
             for arr, ref in enumerate((f_ref, g_ref))
+            if side == 0
         ]
         for copy in copies:
             copy.start()
@@ -215,8 +216,10 @@
             for arr in range(2):
                 parts = []
                 for level in range(levels):
-                    parts.append(tokens[arr, b, level])
-                    if side == 1:
+                    if side == 0:
+                        parts.append(tokens[arr, b, level])
+                    else:
+                        parts.append((f_ref, g_ref)[arr][b, level, start : start + kept])
                         parts.append(lon_ref[arr, b, level])
                 rim = rim_ref[arr, b]
                 if side == 1:
@@ -254,11 +257,13 @@
     if side == 0:
         pick = pick[:, :RIM]
     halos = (rim_in,) if side == 0 else (rim_in, lon_in, cor_in)
+    tokens = (in_hbm(f), in_hbm(g)) if side == 0 else (f, g)
     tall = jax.ShapeDtypeStruct((HALF, width), BF)
     return pl.pallas_call(
         functools.partial(project_kernel, side),
         grid=(QUADS,),
-        in_specs=[SCALARS, full(own), full(pick), IN_HBM, IN_HBM]
+        in_specs=[SCALARS, full(own), full(pick)]
+        + ([IN_HBM, IN_HBM] if side == 0 else [full(f), full(g)])
         + [
             pl.BlockSpec((width, cols), lambda n: (0, n)),
             pl.BlockSpec((width, cols), lambda n: (0, QUADS + n)),
@@ -275,13 +280,13 @@
         out_shape=[pltpu.HBM((HALF, width), BF), tall, jax.ShapeDtypeStruct((width, HALF), BF)] + [tall] * 4,
         scratch_shapes=[
             pltpu.VMEM((HALF, width), BF),
-            pltpu.VMEM((2, samples, levels, kept, width), BF),
+            pltpu.VMEM((2, samples, levels, kept if side == 0 else 16, width), BF),
             pltpu.SemaphoreType.DMA((2,)),
         ],
         compiler_params=params(20),
         cost_estimate=cost(9),
         name="project",
-    )(pos, own, pick, in_hbm(f), in_hbm(g), w_qkv, w_qkv, w_qkv, w_out, *halos)
+    )(pos, own, pick, *tokens, w_qkv, w_qkv, w_qkv, w_out, *halos)
 
 
 def attention_kernel(quads, pos_ref, bias_ref, *rest):

time: 153 us -> 152 us (level)
  Pallas kernels: 73.7 us -> 71.9 us
    pallas_call x2, Pallas kernels: 21.7 us -> 19.9 us  [project(): pl.pallas_call(functools.partial(project_kernel, side), grid=(QUADS,), in...]
    unnamed x86 -> x90, local copies, waits for them, and re-layouts: 4.64 us -> 4.64 us
where the time goes in v2:
time: 152 us; the launch traced here: 151 us
  Pallas kernels  71.9 us (47%)
  waiting for transfers between devices  34.5 us (23%)
  starting transfers between devices  30.7 us (20%)
  local copies, waits for them, and re-layouts  7.59 us (5%)
  other arithmetic  4.73 us (3%)
  between operations  1.91 us (1%)
    pallas_call x3, Pallas kernels, attention(): pl.pallas_call(functools.partial(attention_kernel, quads), grid=(count,),...  30 us
    ppermute x19, waiting for transfers between devices, to_distance(): return lax.ppermute(value, 'lon', pairs)  24.7 us
    ppermute x19, starting transfers between devices, to_distance(): return lax.ppermute(value, 'lon', pairs)  22.2 us
    pallas_call x2, Pallas kernels, project(): pl.pallas_call(functools.partial(project_kernel, side), grid=(QUADS,), in...  19.9 us
    pallas_call x2, Pallas kernels, outputs(): pl.pallas_call(functools.partial(output_kernel, side), grid=(QUADS,), in_...  15.5 us
    ppermute x5, waiting for transfers between devices, swapped(): return lax.ppermute(value, axis, [(0, 1), (1, 0)])  9.03 us
    ppermute x1, starting transfers between devices, shifted_both(): return lax.ppermute(value, ('lon', 'lat'), pairs)  5.06 us
    unnamed x90, local copies, waits for them, and re-layouts  4.64 us
  transfers between devices with their start and end apart: 30, of which 13 were waited for; matrix products, arithmetic and copies ran while one was open for 3% of the time, Pallas kernels for 28%

profile of v2, /device:TPU:64, one launch (start us, length us, event | category | flops | bytes accessed | tf_op | source)
XLA Modules:
  0.0 151.4 jit_solution(2492541581894066493)
XLA Ops:
  0.7 3.6 %strips.1 = (bf16[2,2,3,16,1024]{4,3,2,1,0:T(8,128)(2,1)}, bf16[2,2,128,1024]{3,2,1,0:T(8,128)(2,1)}, bf16[2,2,16,1024]{3,2,1,0:T(8,128)(2,1)}) custom-call(bf16[144,480]{1,0:T(8,128)(2,1)} %constant.132.clone.pick_ref, bf16[2,3,160,1024]{3,2,1,0:T(8,128)(2,1)} %bitcast.42, bf16[2,3,160,1024]{3,2,1,0:T(8,128)(2,1)} %bitcast.45), custom_call_target="tpu_custom_call" | custom-call | flops 3300000000 | bytes 1000000 | tf_op jit(solution)/shard_map/strips/pallas_call | solution.py:181
  4.3 5.1 %collective-permute-start.2 = (bf16[2,2,16,1024]{3,2,1,0:T(8,128)(2,1)}, bf16[2,2,16,1024]{3,2,1,0:T(8,128)(2,1)S(1)}, u32[]{:S(2)}, u32[]{:S(2)}) collective-permute-start(bf16[2,2,16,1024]{3,2,1,0:T(8,128)(2,1)} %get-tuple-element.103), channel_id=1, source_target_pairs={{0,126},{2,124},{4,2},{6,0},{8,6},{10,4},{12,10},{14,8},{16,14},{1... | collective-permute-start | bytes 393224 | tf_op jit(solution)/shard_map/ppermute | solution.py:647
  10.8 2.8 %copy-done = bf16[1024,3072]{1,0:T(8,128)(2,1)S(1)} copy-done((bf16[1024,3072]{1,0:T(8,128)(2,1)S(1)}, bf16[1024,3072]{1,0:T(8,128)(2,1)}, u32[]{:S(2)}) %copy-start) | copy-done | bytes 6291480
  15.3 10.4 %project.2 = (bf16[512,1024]{1,0:T(8,128)(2,1)}, bf16[512,1024]{1,0:T(8,128)(2,1)S(1)}, bf16[1024,512]{1,0:T(8,128)(2,1)S(1)}, bf16[512,1024]{1,0:T(8,128)(2,1)S...) custom-call(s32[2]{0:T(128)S(1)} %pad_add_fusion.1.pos_ref, ...), custom_call_target="tpu_custom_call" | custom-call | flops 9900000256 | bytes 1000000 | tf_op jit(solution)/shard_map/project/pallas_call | solution.py:262
  25.9 9.4 %project.3 = (bf16[512,1024]{1,0:T(8,128)(2,1)}, bf16[512,1024]{1,0:T(8,128)(2,1)S(1)}, bf16[1024,512]{1,0:T(8,128)(2,1)S(1)}, bf16[512,1024]{1,0:T(8,128)(2,1)S...) custom-call(s32[2]{0:T(128)S(1)} %pad_add_fusion.1.pos_ref, ...), custom_call_target="tpu_custom_call" | custom-call | flops 9900000256 | bytes 1000000 | tf_op jit(solution)/shard_map/project/pallas_call | solution.py:262
  35.4 15.9 %attention.3 = (bf16[1024,512]{1,0:T(8,128)(2,1)}, bf16[1024,512]{1,0:T(8,128)(2,1)}, bf16[1024,512]{1,0:T(8,128)(2,1)}, bf16[1024,512]{1,0:T(8,128)(2,1)}, bf16...) custom-call(s32[2]{0:T(128)S(1)} %pad_add_fusion.1.pos_ref, ...), custom_call_target="tpu_custom_call" | custom-call | flops 24199999488 | bytes 1000000 | tf_op jit(solution)/shard_map/attention/pallas_call | solution.py:491
  52.0 3.2 %collective-permute-done.3 = bf16[1024,768]{1,0:T(8,128)(2,1)} collective-permute-done((bf16[1024,768]{1,0:T(8,128)(2,1)}, bf16[1024,768]{1,0:T(8,128)(2,1)}, u32[]{:S(2)}, u32[]{:S(2)}) %collective-permute-start.3) | collective-permute-done | bytes 1572896 | tf_op jit(solution)/shard_map/ppermute | solution.py:667
  59.7 7.1 %attention.4 = (bf16[1024,256]{1,0:T(8,128)(2,1)S(1)}, bf16[1024,256]{1,0:T(8,128)(2,1)S(1)}, bf16[1024,256]{1,0:T(8,128)(2,1)S(1)}, bf16[1024,256]{1,0:T(8,128)...) custom-call(s32[2]{0:T(128)S(1)} %pad_add_fusion.1.pos_ref, ...), custom_call_target="tpu_custom_call" | custom-call | flops 12099999744 | bytes 1000000 | tf_op jit(solution)/shard_map/attention/pallas_call | solution.py:491
  67.0 3.2 %collective-permute-start.6 = (bf16[256,768]{1,0:T(8,128)(2,1)S(1)}, bf16[256,768]{1,0:T(8,128)(2,1)S(1)}, u32[]{:S(2)}, u32[]{:S(2)}) collective-permute-start(bf16[256,768]{1,0:T(8,128)(2,1)S(1)} %pad_maximum_fusion.1), channel_id=1, source_target_pairs={{0,32},{4,36},{8,40},{12,44},{16,48},{20,52},{24,56},{28,60},{32,6... | collective-permute-start | bytes 1179656 | tf_op jit(solution)/shard_map/ppermute | solution.py:675
  70.2 7.1 %attention.5 = (bf16[1024,256]{1,0:T(8,128)(2,1)S(1)}, bf16[1024,256]{1,0:T(8,128)(2,1)S(1)}, bf16[1024,256]{1,0:T(8,128)(2,1)S(1)}, bf16[1024,256]{1,0:T(8,128)...) custom-call(s32[2]{0:T(128)S(1)} %pad_add_fusion.1.pos_ref, ...), custom_call_target="tpu_custom_call" | custom-call | flops 12099999744 | bytes 1000000 | tf_op jit(solution)/shard_map/attention/pallas_call | solution.py:491
  78.3 2.2 %collective-permute-done.7 = bf16[256,768]{1,0:T(8,128)(2,1)S(1)} collective-permute-done((bf16[256,768]{1,0:T(8,128)(2,1)S(1)}, bf16[256,768]{1,0:T(8,128)(2,1)S(1)}, u32[]{:S(2)}, u32[]{:S(2)}) %collective-permute-start.7) | collective-permute-done | bytes 393248 | tf_op jit(solution)/shard_map/ppermute | solution.py:675
  86.1 2.0 %collective-permute-start.11 = (bf16[128,512]{1,0:T(8,128)(2,1)S(1)}, bf16[128,512]{1,0:T(8,128)(2,1)S(1)}, u32[]{:S(2)}, u32[]{:S(2)}) collective-permute-start(bf16[128,512]{1,0:T(8,128)(2,1)S(1)} %get-tuple-element.223), channel_id=1, source_target_pairs={{0,4},{4,8},{8,12},{12,0},{16,20},{20,24},{24,28},{28,16},{32,36},... | collective-permute-start | bytes 393224 | tf_op jit(solution)/shard_map/ppermute | solution.py:675
  88.5 3.0 %collective-permute-start.13 = (bf16[128,768]{1,0:T(8,128)(2,1)S(1)}, bf16[128,768]{1,0:T(8,128)(2,1)S(1)}, u32[]{:S(2)}, u32[]{:S(2)}) collective-permute-start(bf16[128,768]{1,0:T(8,128)(2,1)S(1)} %get-tuple-element.216), channel_id=1, source_target_pairs={{0,32},{4,36},{8,40},{12,44},{16,48},{20,52},{24,56},{28,60},{32,6... | collective-permute-start | bytes 589832 | tf_op jit(solution)/shard_map/ppermute | solution.py:675
  91.6 7.8 %outputs.2 = (bf16[2,3,64,1024]{3,2,1,0:T(8,128)(2,1)S(1)}, bf16[2,3,64,1024]{3,2,1,0:T(8,128)(2,1)S(1)}, bf16[2,2,64,1024]{3,2,1,0:T(8,128)(2,1)S(1)}, bf16[2,2,3,16,1024]{4,3,2,1,0:T(8,128)(2,1)S(1)}) custom-call(bf16[240,256]{1,0:T(8,128)(2,1)S(1)} %copy-done.7, bf16[64,128]{1,0:T(8,128)(2,1)S(1)} %copy-done.12, bf16[512,1024]{1,0:T(8,128)(2,1)S(1)} %copy-done.14, ...), custom_call_target="tpu_custom_call" | custom-call | flops 8800000000 | bytes 1000000 | tf_op jit(solution)/shard_map/outputs/pallas_call | solution.py:562
  103.0 2.0 %collective-permute-start.17 = (bf16[256,512]{1,0:T(8,128)(2,1)S(1)}, bf16[256,512]{1,0:T(8,128)(2,1)S(1)}, u32[]{:S(2)}, u32[]{:S(2)}) collective-permute-start(bf16[256,512]{1,0:T(8,128)(2,1)S(1)} %pad_maximum_fusion.11), channel_id=1, source_target_pairs={{0,12},{4,0},{8,4},{12,8},{16,28},{20,16},{24,20},{28,24},{32,44},... | collective-permute-start | bytes 786440 | tf_op jit(solution)/shard_map/ppermute | solution.py:675
  105.0 2.9 %collective-permute-start.18 = (bf16[256,768]{1,0:T(8,128)(2,1)S(1)}, bf16[256,768]{1,0:T(8,128)(2,1)S(1)}, u32[]{:S(2)}, u32[]{:S(2)}) collective-permute-start(bf16[256,768]{1,0:T(8,128)(2,1)S(1)} %pad_maximum_fusion.7), channel_id=1, source_target_pairs={{0,32},{4,36},{8,40},{12,44},{16,48},{20,52},{24,56},{28,60},{32,6... | collective-permute-start | bytes 1179656 | tf_op jit(solution)/shard_map/ppermute | solution.py:675
  108.0 7.8 %outputs.3 = (bf16[2,3,80,1024]{3,2,1,0:T(8,128)(2,1)S(1)}, bf16[2,3,80,1024]{3,2,1,0:T(8,128)(2,1)S(1)}, bf16[2,2,64,1024]{3,2,1,0:T(8,128)(2,1)S(1)}) custom-call(bf16[240,256]{1,0:T(8,128)(2,1)S(1)} %copy-done.7, bf16[64,128]{1,0:T(8,128)(2,1)S(1)} %copy-done.12, bf16[512,1024]{1,0:T(8,128)(2,1)S(1)} %copy-done.23, bf16[512,1024]{1,0:T(8,128)(2,1)S(1)} %copy-done.25, ...), custom_call_target="tpu_custom_call" | custom-call | flops 8800000000 | bytes 1000000 | tf_op jit(solution)/shard_map/outputs/pallas_call | solution.py:562
  116.1 2.2 %collective-permute-done.19 = bf16[256,768]{1,0:T(8,128)(2,1)S(1)} collective-permute-done((bf16[256,768]{1,0:T(8,128)(2,1)S(1)}, bf16[256,768]{1,0:T(8,128)(2,1)S(1)}, u32[]{:S(2)}, u32[]{:S(2)}) %collective-permute-start.19) | collective-permute-done | bytes 393248 | tf_op jit(solution)/shard_map/ppermute | solution.py:675
  122.7 9.1 %collective-permute-done.23 = bf16[64,512]{1,0:T(8,128)(2,1)S(1)} collective-permute-done((bf16[64,512]{1,0:T(8,128)(2,1)S(1)}, bf16[64,512]{1,0:T(8,128)(2,1)S(1)}, u32[]{:S(2)}, u32[]{:S(2)}) %collective-permute-start.23) | collective-permute-done | bytes 65568 | tf_op jit(solution)/shard_map/ppermute | solution.py:675
  131.9 2.2 %collective-permute-done.20 = bf16[64,1536]{1,0:T(8,128)(2,1)S(1)} collective-permute-done((bf16[64,1536]{1,0:T(8,128)(2,1)S(1)}, bf16[64,1536]{1,0:T(8,128)(2,1)S(1)}, u32[]{:S(2)}, u32[]{:S(2)}) %collective-permute-start.20) | collective-permute-done | bytes 196640 | tf_op jit(solution)/shard_map/ppermute | solution.py:675
  134.1 4.8 %collective-permute-done.21 = bf16[64,1536]{1,0:T(8,128)(2,1)S(1)} collective-permute-done((bf16[64,1536]{1,0:T(8,128)(2,1)S(1)}, bf16[64,1536]{1,0:T(8,128)(2,1)S(1)}, u32[]{:S(2)}, u32[]{:S(2)}) %collective-permute-start.21) | collective-permute-done | bytes 196640 | tf_op jit(solution)/shard_map/ppermute | solution.py:675
  140.1 2.6 %merge.1 = (bf16[2,3,160,1024]{3,2,1,0:T(8,128)(2,1)}, bf16[2,3,160,1024]{3,2,1,0:T(8,128)(2,1)}) custom-call(bf16[3,80,64]{2,1,0:T(8,128)(2,1)S(1)} %copy-done.9, bf16[3,64,64]{2,1,0:T(8,128)(2,1)S(1)} %copy-done.10, bf16[2,3,80,1024]{3,2,1,0:T(8,128)(2,1)S(1)} %get-tuple-element.175.y0, bf16[2,3,80,1024]{3,2,1,0:T(8,128)(2,1)S(1)} %get-tuple-element.176.g0, ...), custom_call_target="tpu_custom_call" | custom-call | flops 4400000000 | bytes 1000000 | tf_op jit(solution)/shard_map/merge/pallas_call | solution.py:620
  142.7 2.9 %collective-permute-done.26 = bf16[32,2048]{1,0:T(8,128)(2,1)S(1)} collective-permute-done((bf16[32,2048]{1,0:T(8,128)(2,1)S(1)}, bf16[32,2048]{1,0:T(8,128)(2,1)S(1)}, u32[]{:S(2)}, u32[]{:S(2)}) %collective-permute-start.26) | collective-permute-done | bytes 131104 | tf_op jit(solution)/shard_map/ppermute | solution.py:675
  147.1 3.0 %collective-permute-done.29 = bf16[32,1024]{1,0:T(8,128)(2,1)S(1)} collective-permute-done((bf16[32,1024]{1,0:T(8,128)(2,1)S(1)}, bf16[32,1024]{1,0:T(8,128)(2,1)S(1)}, u32[]{:S(2)}, u32[]{:S(2)}) %collective-permute-start.29) | collective-permute-done | bytes 65568 | tf_op jit(solution)/shard_map/ppermute | solution.py:667
  (206 shorter events, 27.2 us)
Async XLA Ops:
  4.3 21.5 %collective-permute-start.2 = (bf16[2,2,16,1024]{3,2,1,0:T(8,128)(2,1)}, bf16[2,2,16,1024]{3,2,1,0:T(8,128)(2,1)S(1)}, u32[]{:S(2)}, u32[]{:S(2)}) collective-permute-start(bf16[2,2,16,1024]{3,2,1,0:T(8,128)(2,1)} %get-tuple-element.103), channel_id=1, source_target_pairs={{0,126},{2,124},{4,2},{6,0},{8,6},{10,4},{12,10},{14,8},{16,14},{1... | collective-permute-start | bytes 393224 | tf_op jit(solution)/shard_map/ppermute | solution.py:647
  9.4 16.5 %collective-permute-start.1 = (bf16[2,2,3,16,1024]{4,3,2,1,0:T(8,128)(2,1)}, bf16[2,2,3,16,1024]{4,3,2,1,0:T(8,128)(2,1)}, u32[]{:S(2)}, u32[]{:S(2)}) collective-permute-start(bf16[2,2,3,16,1024]{4,3,2,1,0:T(8,128)(2,1)} %get-tuple-element.102), channel_id=1, source_target_pairs={{0,124},{4,0},{8,4},{12,8},{16,12},{20,16},{24,20},{28,24},{32,28}... | collective-permute-start | bytes 1179656 | tf_op jit(solution)/shard_map/ppermute | solution.py:637
  51.6 29.0 %collective-permute-start.10 = (bf16[512,512]{1,0:T(8,128)(2,1)S(1)}, bf16[512,512]{1,0:T(8,128)(2,1)S(1)}, u32[]{:S(2)}, u32[]{:S(2)}) collective-permute-start(bf16[512,512]{1,0:T(8,128)(2,1)S(1)} %get-tuple-element.134), channel_id=1, source_target_pairs={{0,2},{2,0},{1,3},{3,1},{4,6},{6,4},{5,7},{7,5},{8,10},{10,8},{9,1... | collective-permute-start | bytes 1572872 | tf_op jit(solution)/shard_map/ppermute | solution.py:667
  57.4 9.4 %collective-permute-start.5 = (bf16[128,768]{1,0:T(8,128)(2,1)S(1)}, bf16[128,768]{1,0:T(8,128)(2,1)S(1)}, u32[]{:S(2)}, u32[]{:S(2)}) collective-permute-start(bf16[128,768]{1,0:T(8,128)(2,1)S(1)} %get-tuple-element.217), channel_id=1, source_target_pairs={{0,96},{4,100},{8,104},{12,108},{16,112},{20,116},{24,120},{28,124... | collective-permute-start | bytes 589832 | tf_op jit(solution)/shard_map/ppermute | solution.py:675
  57.7 9.1 %collective-permute-start.4 = (bf16[128,768]{1,0:T(8,128)(2,1)S(1)}, bf16[128,768]{1,0:T(8,128)(2,1)S(1)}, u32[]{:S(2)}, u32[]{:S(2)}) collective-permute-start(bf16[128,768]{1,0:T(8,128)(2,1)S(1)} %get-tuple-element.218), channel_id=1, source_target_pairs={{0,32},{4,36},{8,40},{12,44},{16,48},{20,52},{24,56},{28,60},{32,6... | collective-permute-start | bytes 589832 | tf_op jit(solution)/shard_map/ppermute | solution.py:675
  67.0 11.3 %collective-permute-start.6 = (bf16[256,768]{1,0:T(8,128)(2,1)S(1)}, bf16[256,768]{1,0:T(8,128)(2,1)S(1)}, u32[]{:S(2)}, u32[]{:S(2)}) collective-permute-start(bf16[256,768]{1,0:T(8,128)(2,1)S(1)} %pad_maximum_fusion.1), channel_id=1, source_target_pairs={{0,32},{4,36},{8,40},{12,44},{16,48},{20,52},{24,56},{28,60},{32,6... | collective-permute-start | bytes 1179656 | tf_op jit(solution)/shard_map/ppermute | solution.py:675
  70.2 10.4 %collective-permute-start.7 = (bf16[256,768]{1,0:T(8,128)(2,1)S(1)}, bf16[256,768]{1,0:T(8,128)(2,1)S(1)}, u32[]{:S(2)}, u32[]{:S(2)}) collective-permute-start(bf16[256,768]{1,0:T(8,128)(2,1)S(1)} %pad_maximum_fusion.2), channel_id=1, source_target_pairs={{0,96},{4,100},{8,104},{12,108},{16,112},{20,116},{24,120},{28,124... | collective-permute-start | bytes 1179656 | tf_op jit(solution)/shard_map/ppermute | solution.py:675
  86.0 13.5 %collective-permute-start.12 = (bf16[128,512]{1,0:T(8,128)(2,1)S(1)}, bf16[128,512]{1,0:T(8,128)(2,1)S(1)}, u32[]{:S(2)}, u32[]{:S(2)}) collective-permute-start(bf16[128,512]{1,0:T(8,128)(2,1)S(1)} %get-tuple-element.222), channel_id=1, source_target_pairs={{0,12},{4,0},{8,4},{12,8},{16,28},{20,16},{24,20},{28,24},{32,44},... | collective-permute-start | bytes 393224 | tf_op jit(solution)/shard_map/ppermute | solution.py:675
  86.1 13.4 %collective-permute-start.11 = (bf16[128,512]{1,0:T(8,128)(2,1)S(1)}, bf16[128,512]{1,0:T(8,128)(2,1)S(1)}, u32[]{:S(2)}, u32[]{:S(2)}) collective-permute-start(bf16[128,512]{1,0:T(8,128)(2,1)S(1)} %get-tuple-element.223), channel_id=1, source_target_pairs={{0,4},{4,8},{8,12},{12,0},{16,20},{20,24},{24,28},{28,16},{32,36},... | collective-permute-start | bytes 393224 | tf_op jit(solution)/shard_map/ppermute | solution.py:675
  88.2 11.4 %collective-permute-start.14 = (bf16[128,768]{1,0:T(8,128)(2,1)S(1)}, bf16[128,768]{1,0:T(8,128)(2,1)S(1)}, u32[]{:S(2)}, u32[]{:S(2)}) collective-permute-start(bf16[128,768]{1,0:T(8,128)(2,1)S(1)} %get-tuple-element.215), channel_id=1, source_target_pairs={{0,96},{4,100},{8,104},{12,108},{16,112},{20,116},{24,120},{28,124... | collective-permute-start | bytes 589832 | tf_op jit(solution)/shard_map/ppermute | solution.py:675
  88.5 11.1 %collective-permute-start.13 = (bf16[128,768]{1,0:T(8,128)(2,1)S(1)}, bf16[128,768]{1,0:T(8,128)(2,1)S(1)}, u32[]{:S(2)}, u32[]{:S(2)}) collective-permute-start(bf16[128,768]{1,0:T(8,128)(2,1)S(1)} %get-tuple-element.216), channel_id=1, source_target_pairs={{0,32},{4,36},{8,40},{12,44},{16,48},{20,52},{24,56},{28,60},{32,6... | collective-permute-start | bytes 589832 | tf_op jit(solution)/shard_map/ppermute | solution.py:675
  101.7 14.1 %collective-permute-start.16 = (bf16[256,512]{1,0:T(8,128)(2,1)S(1)}, bf16[256,512]{1,0:T(8,128)(2,1)S(1)}, u32[]{:S(2)}, u32[]{:S(2)}) collective-permute-start(bf16[256,512]{1,0:T(8,128)(2,1)S(1)} %pad_maximum_fusion.10), channel_id=1, source_target_pairs={{0,4},{4,8},{8,12},{12,0},{16,20},{20,24},{24,28},{28,16},{32,36},... | collective-permute-start | bytes 786440 | tf_op jit(solution)/shard_map/ppermute | solution.py:675
  103.0 12.8 %collective-permute-start.17 = (bf16[256,512]{1,0:T(8,128)(2,1)S(1)}, bf16[256,512]{1,0:T(8,128)(2,1)S(1)}, u32[]{:S(2)}, u32[]{:S(2)}) collective-permute-start(bf16[256,512]{1,0:T(8,128)(2,1)S(1)} %pad_maximum_fusion.11), channel_id=1, source_target_pairs={{0,12},{4,0},{8,4},{12,8},{16,28},{20,16},{24,20},{28,24},{32,44},... | collective-permute-start | bytes 786440 | tf_op jit(solution)/shard_map/ppermute | solution.py:675
  105.0 11.0 %collective-permute-start.18 = (bf16[256,768]{1,0:T(8,128)(2,1)S(1)}, bf16[256,768]{1,0:T(8,128)(2,1)S(1)}, u32[]{:S(2)}, u32[]{:S(2)}) collective-permute-start(bf16[256,768]{1,0:T(8,128)(2,1)S(1)} %pad_maximum_fusion.7), channel_id=1, source_target_pairs={{0,32},{4,36},{8,40},{12,44},{16,48},{20,52},{24,56},{28,60},{32,6... | collective-permute-start | bytes 1179656 | tf_op jit(solution)/shard_map/ppermute | solution.py:675
  108.0 10.3 %collective-permute-start.19 = (bf16[256,768]{1,0:T(8,128)(2,1)S(1)}, bf16[256,768]{1,0:T(8,128)(2,1)S(1)}, u32[]{:S(2)}, u32[]{:S(2)}) collective-permute-start(bf16[256,768]{1,0:T(8,128)(2,1)S(1)} %pad_maximum_fusion.8), channel_id=1, source_target_pairs={{0,96},{4,100},{8,104},{12,108},{16,112},{20,116},{24,120},{28,124... | collective-permute-start | bytes 1179656 | tf_op jit(solution)/shard_map/ppermute | solution.py:675
  115.7 24.4 %collective-permute-start.28 = (bf16[2,2,3,16,1024]{4,3,2,1,0:T(8,128)(2,1)S(1)}, bf16[2,2,3,16,1024]{4,3,2,1,0:T(8,128)(2,1)S(1)}, u32[]{:S(2)}, u32[]{:S(2)}) collective-permute-start(bf16[2,2,3,16,1024]{4,3,2,1,0:T(8,128)(2,1)S(1)} %patch.1), channel_id=1, source_target_pairs={{0,4},{4,8},{8,12},{12,16},{16,20},{20,24},{24,28},{28,32},{32,36}... | collective-permute-start | bytes 1179656 | tf_op jit(solution)/shard_map/ppermute | solution.py:637
  118.6 13.1 %collective-permute-start.23 = (bf16[64,512]{1,0:T(8,128)(2,1)S(1)}, bf16[64,512]{1,0:T(8,128)(2,1)S(1)}, u32[]{:S(2)}, u32[]{:S(2)}) collective-permute-start(bf16[64,512]{1,0:T(8,128)(2,1)S(1)} %get-tuple-element.219), channel_id=1, source_target_pairs={{0,32},{4,36},{8,40},{12,44},{16,48},{20,52},{24,56},{28,60},{32,6... | collective-permute-start | bytes 196616 | tf_op jit(solution)/shard_map/ppermute | solution.py:675
  120.2 11.6 %collective-permute-start.25 = (bf16[64,512]{1,0:T(8,128)(2,1)S(1)}, bf16[64,512]{1,0:T(8,128)(2,1)S(1)}, u32[]{:S(2)}, u32[]{:S(2)}) collective-permute-start(bf16[64,512]{1,0:T(8,128)(2,1)S(1)} %get-tuple-element.220), channel_id=1, source_target_pairs={{0,96},{4,100},{8,104},{12,108},{16,112},{20,116},{24,120},{28,124... | collective-permute-start | bytes 196616 | tf_op jit(solution)/shard_map/ppermute | solution.py:675
  120.7 11.1 %collective-permute-start.24 = (bf16[64,512]{1,0:T(8,128)(2,1)S(1)}, bf16[64,512]{1,0:T(8,128)(2,1)S(1)}, u32[]{:S(2)}, u32[]{:S(2)}) collective-permute-start(bf16[64,512]{1,0:T(8,128)(2,1)S(1)} %get-tuple-element.221), channel_id=1, source_target_pairs={{0,64},{4,68},{8,72},{12,76},{16,80},{20,84},{24,88},{28,92},{32,9... | collective-permute-start | bytes 196616 | tf_op jit(solution)/shard_map/ppermute | solution.py:675
  122.6 11.6 %collective-permute-start.20 = (bf16[64,1536]{1,0:T(8,128)(2,1)S(1)}, bf16[64,1536]{1,0:T(8,128)(2,1)S(1)}, u32[]{:S(2)}, u32[]{:S(2)}) collective-permute-start(bf16[64,1536]{1,0:T(8,128)(2,1)S(1)} %pad_maximum_fusion.12), channel_id=1, source_target_pairs={{0,4},{4,8},{8,12},{12,0},{16,20},{20,24},{24,28},{28,16},{32,36},... | collective-permute-start | bytes 589832 | tf_op jit(solution)/shard_map/ppermute | solution.py:675
  131.8 7.2 %collective-permute-start.21 = (bf16[64,1536]{1,0:T(8,128)(2,1)S(1)}, bf16[64,1536]{1,0:T(8,128)(2,1)S(1)}, u32[]{:S(2)}, u32[]{:S(2)}) collective-permute-start(bf16[64,1536]{1,0:T(8,128)(2,1)S(1)} %pad_maximum_fusion.13), channel_id=1, source_target_pairs={{0,8},{4,12},{8,0},{12,4},{16,24},{20,28},{24,16},{28,20},{32,40},... | collective-permute-start | bytes 589832 | tf_op jit(solution)/shard_map/ppermute | solution.py:675
  131.8 7.2 %collective-permute-start.22 = (bf16[64,1536]{1,0:T(8,128)(2,1)S(1)}, bf16[64,1536]{1,0:T(8,128)(2,1)S(1)}, u32[]{:S(2)}, u32[]{:S(2)}) collective-permute-start(bf16[64,1536]{1,0:T(8,128)(2,1)S(1)} %pad_maximum_fusion.14), channel_id=1, source_target_pairs={{0,12},{4,0},{8,4},{12,8},{16,28},{20,16},{24,20},{28,24},{32,44},... | collective-permute-start | bytes 589832 | tf_op jit(solution)/shard_map/ppermute | solution.py:675
  131.8 8.3 %collective-permute-start.27 = (bf16[2,2,64,1024]{3,2,1,0:T(8,128)(2,1)S(1)}, bf16[2,2,64,1024]{3,2,1,0:T(8,128)(2,1)S(1)}, u32[]{:S(2)}, u32[]{:S(2)}) collective-permute-start(bf16[2,2,64,1024]{3,2,1,0:T(8,128)(2,1)S(1)} %get-tuple-element.179), channel_id=1, source_target_pairs={{0,2},{2,0},{1,3},{3,1},{4,6},{6,4},{5,7},{7,5},{8,10},{10,8},{9,1... | collective-permute-start | bytes 1572872 | tf_op jit(solution)/shard_map/ppermute | solution.py:637
  139.1 6.6 %collective-permute-start.26 = (bf16[32,2048]{1,0:T(8,128)(2,1)S(1)}, bf16[32,2048]{1,0:T(8,128)(2,1)S(1)}, u32[]{:S(2)}, u32[]{:S(2)}) collective-permute-start(bf16[32,2048]{1,0:T(8,128)(2,1)S(1)} %fusion), channel_id=1, source_target_pairs={{0,16},{4,20},{8,24},{12,28},{16,0},{20,4},{24,8},{28,12},{32,48},... | collective-permute-start | bytes 393224 | tf_op jit(solution)/shard_map/ppermute | solution.py:675
  (52 other events, 408.2 us)
